TPU v7x, 32 devices: a whole 2x2x4 slice. The times are simulated.
32 devices in a mesh: grp: 4 (over y, core), brick: 8 (over z, x).
Axes of the slice: x: 2, y: 2, z: 4, core: 2. Of those that a mesh axis runs over, the one named last changes fastest.
Arguments:
- right_side: float32 [3, 64, 128, 128], P(None, 'grp', 'brick'), may hold values from -24 to 24
- stiffness: float32 [64, 128, 128], P('grp', 'brick'), may hold values from 1 to 10
- reaction: float32 [64, 128, 128], P('grp', 'brick'), may hold values from 0.1 to 1
Outputs:
- correction: float32 [3, 64, 128, 128], P(None, 'grp', 'brick')
All inputs are finite; a program needn't handle non-finite values.
Results may differ from a plain program's by a relative error of at most 0.00025.
Values sent between devices are 32-bit elements; how exact they have to be, the bound alone decides.
A program may use at most 128 MiB of HBM per device.

v0:
```python
import jax
import jax.numpy as jnp
from jax import lax
from jax.sharding import PartitionSpec as P

LEVELS = 4


BETA = 1.0
THETA = 1.5
DELTA = 1.0
SIGMA = 1.5


def with_halo(cells, sides, width):
    for axis, dim in sides:
        count = lax.axis_size(axis)
        ends = count - 1
        head = lax.slice_in_dim(cells, 0, width, axis=dim)
        tail = lax.slice_in_dim(cells, cells.shape[dim] - width, cells.shape[dim], axis=dim)
        cells = jnp.concatenate(
            [
                lax.ppermute(tail, axis, [(i, (i + 1) % count) for i in range(ends)]),
                cells,
                lax.ppermute(head, axis, [((i + 1) % count, i) for i in range(ends)]),
            ],
            axis=dim,
        )
    return cells


def rate_list():
    rates = [1.0 / SIGMA]
    for number in range(3):
        rates.append(1.0 / (2.0 * SIGMA - rates[-1]))
    return rates


def advance(step, old, resid, inverse):
    rates = rate_list()
    return rates[step] * rates[step - 1] * old + 2.0 * rates[step] / DELTA * (inverse * resid)


def offset_of(axis, sign):
    return tuple((sign if index == axis else 0 for index in range(3)))


def view(array, shift, rows, cols, depth):
    return array[
        ...,
        1 + shift[0] : 1 + shift[0] + rows,
        1 + shift[1] : 1 + shift[1] + cols,
        1 + shift[2] : 1 + shift[2] + depth,
    ]


def face_total(stiff, rows, cols, depth):
    centre = view(stiff, (0, 0, 0), rows, cols, depth)
    total = jnp.zeros_like(centre)
    for axis in range(3):
        total = total + 0.5 * (centre + view(stiff, offset_of(axis, 1), rows, cols, depth))
        total = total + 0.5 * (centre + view(stiff, offset_of(axis, -1), rows, cols, depth))
    return total


def inverse_diagonal(coeff, scale):
    rows = coeff.shape[1] - 2
    cols = coeff.shape[2] - 2
    depth = coeff.shape[3]
    stiff = jnp.pad(coeff[0], ((0, 0), (0, 0), (1, 1)))
    react = coeff[1, 1:-1, 1:-1, :]
    faces = face_total(stiff, rows, cols, depth)
    return (1.0 / (scale * (faces + 2.0 * BETA) + react))[None]


def operate(field, coeff, scale):
    rows = field.shape[1] - 2
    cols = field.shape[2] - 2
    depth = field.shape[3]
    padded = jnp.pad(field, ((0, 0), (0, 0), (0, 0), (1, 1)))
    stiff = jnp.pad(coeff[0], ((0, 0), (0, 0), (1, 1)))
    react = coeff[1, 1:-1, 1:-1, :]
    centre = view(stiff, (0, 0, 0), rows, cols, depth)
    middle = view(padded, (0, 0, 0), rows, cols, depth)
    laplace = jnp.zeros_like(middle)
    for axis in range(3):
        ahead = offset_of(axis, 1)
        behind = offset_of(axis, -1)
        upper = 0.5 * (centre + view(stiff, ahead, rows, cols, depth))
        lower = 0.5 * (centre + view(stiff, behind, rows, cols, depth))
        laplace = laplace + upper * (middle - view(padded, ahead, rows, cols, depth))
        laplace = laplace + lower * (middle - view(padded, behind, rows, cols, depth))

    def divergence(anchor):
        total = jnp.zeros_like(centre)
        for axis in range(3):
            moved = tuple((anchor[index] + offset_of(axis, 1)[index] for index in range(3)))
            total = (
                total
                + view(padded[axis], moved, rows, cols, depth)
                - view(padded[axis], anchor, rows, cols, depth)
            )
        return total

    centre_div = divergence((0, 0, 0))
    parts = []
    for axis in range(3):
        graddiv = divergence(offset_of(axis, -1)) - centre_div
        parts.append(scale * (laplace[axis] + BETA * graddiv) + react * middle[axis])
    return jnp.stack(parts)


def shrink(array):
    comps, rows, cols, depth = array.shape
    blocks = array.reshape(comps, rows // 2, 2, cols // 2, 2, depth // 2, 2)
    return blocks.mean(axis=(2, 4, 6))


def grow(array):
    return jnp.repeat(jnp.repeat(jnp.repeat(array, 2, axis=1), 2, axis=2), 2, axis=3)


def crop(array, have, want):
    margin = have - want
    return array[:, margin:-margin, margin:-margin, :]


def spread(array, width):
    return with_halo(array, (("grp", 1), ("brick", 2)), width)


def relax_plain(source, start, context):
    padded, inverse, scale, group = context
    near_coeff = crop(padded, 2, 1)
    inner_inverse = crop(inverse, 1, 0)
    if start is None:
        resid = source
        state = jnp.zeros_like(source)
    else:
        resid = source - operate(spread(start, 1), near_coeff, scale)
        state = start
    step_dir = inner_inverse * resid / THETA
    for step in range(1, 4):
        state = state + step_dir
        resid = source - operate(spread(state, 1), near_coeff, scale)
        step_dir = advance(step, step_dir, resid, inner_inverse)
    return state + step_dir


def relax(source, start, context):
    return relax_plain(source, start, context)


def on_device(right_side, stiffness, reaction):
    coeff = jnp.stack([stiffness, reaction])
    contexts = []
    group = 1
    for level in range(LEVELS):
        scale = 0.25**level
        if level > 0:
            coeff = shrink(coeff)
        padded = spread(coeff, 2)
        contexts.append((padded, inverse_diagonal(padded, scale), scale, group))
    sources = [right_side]
    saved = []
    source_rims = []
    answer = right_side
    for level in range(LEVELS):
        source = sources[level]
        padded, inverse, scale, group = contexts[level]
        source_rims.append(source)
        smooth = relax(source, None, contexts[level])
        if level < LEVELS - 1:
            saved.append(smooth)
            resid = source - operate(spread(smooth, 1), crop(padded, 2, 1), scale)
            coarse = shrink(resid)
            sources.append(coarse)
        else:
            answer = smooth
    for level in reversed(range(LEVELS - 1)):
        answer = relax(sources[level], saved[level] + grow(answer), contexts[level])
    return answer


def solution(mesh):
    in_specs = (P(None, "grp", "brick", None), P("grp", "brick", None), P("grp", "brick", None))
    out_specs = P(None, "grp", "brick", None)
    return jax.shard_map(
        on_device, mesh=mesh, in_specs=in_specs, out_specs=out_specs, check_vma=False
    )
```

profile of v0, /device:TPU:28, one launch (start us, length us, event | category | flops | bytes accessed | tf_op | source)
XLA Modules:
  0.0 588.2 jit_solution(17373208107201195855)
XLA Ops:
  0.0 10.5 %stack.359 = f32[1,8,2,8,2,64,2]{6,5,4,3,2,1,0:T(8,128)} reshape(f32[16,16,128]{2,1,0:T(8,128)} %param.5) | data formatting | bytes 262144 | tf_op jit(solution)/shard_map/stack | solution.py:155
  10.5 9.7 %stack.358 = f32[1,8,2,8,2,64,2]{6,5,4,3,2,1,0:T(8,128)} reshape(f32[16,16,128]{2,1,0:T(8,128)S(1)} %copy-done.2) | data formatting | bytes 262144 | tf_op jit(solution)/shard_map/stack | solution.py:155
  20.3 7.5 %maximum_reduce_fusion = f32[2,8,8,64]{3,2,1,0:T(8,128)S(1)} fusion(f32[1,8,2,8,2,64,2]{6,5,4,3,2,1,0:T(8,128)} %stack.359, f32[1,8,2,8,2,64,2]{6,5,4,3,2,1,0:T(8,128)} %stack.358), kind=kLoop, calls=%fused_computation | loop fusion | flops 122880 | bytes 294912 | tf_op jit(solution)/shard_map/reduce_sum | solution.py:116
  27.8 3.5 div.104
  37.8 3.2 collective-permute-start.1
  42.9 3.6 collective-permute-start.21
  51.0 3.3 collective-permute-start.3
  56.9 4.2 collective-permute-done.2
  66.6 2.7 collective-permute-done.5
  71.3 3.9 collective-permute-start.7
  80.1 3.0 collective-permute-start.8
  85.1 2.8 collective-permute-start.23
  87.9 3.0 collective-permute-start.22
  91.0 3.7 collective-permute-start.10
  97.4 4.0 collective-permute-done.11
  108.0 3.0 collective-permute-done.13
  112.9 3.9 collective-permute-start.15
  126.2 2.7 collective-permute-done.17
  129.0 2.9 collective-permute-start.18
  131.9 2.9 collective-permute-start.19
  134.9 3.7 collective-permute-done.19
  140.6 26.5 %reshape.145 = f32[3,8,2,8,2,64,2]{6,5,4,3,2,1,0:T(8,128)} reshape(f32[3,16,16,128]{3,2,1,0:T(8,128)S(1)} %maximum_subtract_fusion.4) | data formatting | bytes 786432 | tf_op jit(solution)/shard_map/reshape | solution.py:115
  167.1 9.4 %reduce_sum.54 = f32[3,8,8,64]{3,2,1,0:T(8,128)S(1)} reduce(f32[3,8,2,8,2,64,2]{6,5,4,3,2,1,0:T(8,128)} %reshape.145, f32[]{:T(128)} %constant.22.clone.1), dimensions={2,4,6}, to_apply=%region_0.1 | reduce | flops 86016 | bytes 442372 | tf_op jit(solution)/shard_map/reduce_sum | solution.py:116
  185.5 3.9 collective-permute-start.27
  197.1 2.9 collective-permute-start.43
  200.1 2.9 collective-permute-start.42
  203.1 3.8 collective-permute-start.30
  209.0 4.4 collective-permute-done.31
  223.1 3.9 collective-permute-start.35
  239.4 3.9 collective-permute-start.39
  243.3 4.9 div.102
  252.0 2.9 stack.374
  257.0 3.0 fusion
  266.9 2.8 collective-permute-start.46
  269.8 3.0 collective-permute-start.47
  273.5 2.7 collective-permute-done.47
  283.7 3.9 collective-permute-start.62
  287.7 2.8 collective-permute-start.50
  290.5 3.0 collective-permute-start.51
  294.3 2.7 collective-permute-done.51
  306.3 3.9 collective-permute-start.55
  322.1 3.9 collective-permute-start.59
  338.3 3.9 collective-permute-start.67
  354.0 3.9 collective-permute-start.71
  369.7 3.9 collective-permute-start.75
  385.8 3.9 collective-permute-start.79
  401.6 3.9 collective-permute-start.83
  417.4 3.9 collective-permute-start.87
  433.2 4.1 collective-permute-start.91
  452.4 3.9 collective-permute-start.95
  468.5 3.9 collective-permute-start.99
  484.7 3.9 collective-permute-start.103
  500.9 3.9 collective-permute-start.107
  519.8 2.7 collective-permute-done.109
  524.5 3.9 collective-permute-start.111
  528.4 2.7 collective-permute-done.111
  537.6 2.7 collective-permute-done.113
  542.3 3.9 collective-permute-start.115
  546.2 2.7 collective-permute-done.115
  555.4 2.7 collective-permute-done.117
  560.1 4.2 collective-permute-start.119
  573.4 2.7 collective-permute-done.121
  578.1 3.9 collective-permute-start.123
  582.0 2.7 collective-permute-done.123
  (556 shorter events, 316.6 us)
Async XLA Ops:
  33.5 247.6 %collective-permute-start.61 = (f32[2,2,2,16]{3,2,1,0:T(2,128)S(1)}, f32[2,2,2,16]{3,2,1,0:T(2,128)S(1)}, u32[]{:S(2)}, u32[]{:S(2)}) collective-permute-start(f32[2,2,2,16]{3,2,1,0:T(2,128)S(1)} %broadcast_multiply_fusion.6), channel_id=1, source_target_pairs={{8,0},{16,8},{24,16},{9,1},{17,9},{25,17},{10,2},{18,10},{26,18},{... | collective-permute-start | bytes 1544 | tf_op jit(solution)/shard_map/ppermute | solution.py:25
  35.4 245.7 %collective-permute-start.60 = (f32[2,2,2,16]{3,2,1,0:T(2,128)S(1)}, f32[2,2,2,16]{3,2,1,0:T(2,128)}, u32[]{:S(2)}, u32[]{:S(2)}) collective-permute-start(f32[2,2,2,16]{3,2,1,0:T(2,128)S(1)} %broadcast_multiply_fusion.6), channel_id=1, source_target_pairs={{0,8},{8,16},{16,24},{1,9},{9,17},{17,25},{2,10},{10,18},{18,26},{... | collective-permute-start | bytes 1544 | tf_op jit(solution)/shard_map/ppermute | solution.py:23
  37.8 8.8 %collective-permute-start.1 = (f32[2,2,16,128]{3,2,1,0:T(8,128)S(1)}, f32[2,2,16,128]{3,2,1,0:T(8,128)S(1)}, u32[]{:S(2)}, u32[]{:S(2)}) collective-permute-start(f32[2,2,16,128]{3,2,1,0:T(8,128)S(1)} %get-tuple-element.158), channel_id=1, source_target_pairs={{8,0},{16,8},{24,16},{9,1},{17,9},{25,17},{10,2},{18,10},{26,18},{... | collective-permute-start | bytes 98312 | tf_op jit(solution)/shard_map/ppermute | solution.py:25
  41.0 7.5 %collective-permute-start = (f32[2,2,16,128]{3,2,1,0:T(8,128)S(1)}, f32[2,2,16,128]{3,2,1,0:T(8,128)S(1)}, u32[]{:S(2)}, u32[]{:S(2)}) collective-permute-start(f32[2,2,16,128]{3,2,1,0:T(8,128)S(1)} %get-tuple-element.157), channel_id=1, source_target_pairs={{0,8},{8,16},{16,24},{1,9},{9,17},{17,25},{2,10},{10,18},{18,26},{... | collective-permute-start | bytes 98312 | tf_op jit(solution)/shard_map/ppermute | solution.py:23
  42.9 40.2 %collective-permute-start.21 = (f32[2,2,8,64]{3,2,1,0:T(8,128)S(1)}, f32[2,2,8,64]{3,2,1,0:T(8,128)S(1)}, u32[]{:S(2)}, u32[]{:S(2)}) collective-permute-start(f32[2,2,8,64]{3,2,1,0:T(8,128)S(1)} %get-tuple-element.272), channel_id=1, source_target_pairs={{8,0},{16,8},{24,16},{9,1},{17,9},{25,17},{10,2},{18,10},{26,18},{... | collective-permute-start | bytes 24584 | tf_op jit(solution)/shard_map/ppermute | solution.py:25
  51.0 5.9 %collective-permute-start.3 = (f32[2,20,2,128]{3,2,1,0:T(2,128)S(1)}, f32[2,20,2,128]{3,2,1,0:T(2,128)S(1)}, u32[]{:S(2)}, u32[]{:S(2)}) collective-permute-start(f32[2,20,2,128]{3,2,1,0:T(2,128)S(1)} %get-tuple-element.156), channel_id=1, source_target_pairs={{1,0},{2,1},{3,2},{4,3},{5,4},{6,5},{7,6},{9,8},{10,9},{11,10},{12... | collective-permute-start | bytes 122888 | tf_op jit(solution)/shard_map/ppermute | solution.py:25
  54.3 6.8 %collective-permute-start.2 = (f32[2,20,2,128]{3,2,1,0:T(2,128)S(1)}, f32[2,20,2,128]{3,2,1,0:T(2,128)S(1)}, u32[]{:S(2)}, u32[]{:S(2)}) collective-permute-start(f32[2,20,2,128]{3,2,1,0:T(2,128)S(1)} %get-tuple-element.155), channel_id=1, source_target_pairs={{0,1},{1,2},{2,3},{3,4},{4,5},{5,6},{6,7},{8,9},{9,10},{10,11},{11... | collective-permute-start | bytes 122888 | tf_op jit(solution)/shard_map/ppermute | solution.py:23
  69.4 6.0 %collective-permute-start.6 = (f32[3,18,1,128]{3,2,1,0:T(1,128)S(1)}, f32[3,18,1,128]{3,2,1,0:T(1,128)S(1)}, u32[]{:S(2)}, u32[]{:S(2)}) collective-permute-start(f32[3,18,1,128]{3,2,1,0:T(1,128)S(1)} %get-tuple-element.138), channel_id=1, source_target_pairs={{1,0},{2,1},{3,2},{4,3},{5,4},{6,5},{7,6},{9,8},{10,9},{11,10},{12... | collective-permute-start | bytes 82952 | tf_op jit(solution)/shard_map/ppermute | solution.py:25
  71.3 6.7 %collective-permute-start.7 = (f32[3,18,1,128]{3,2,1,0:T(1,128)S(1)}, f32[3,18,1,128]{3,2,1,0:T(1,128)S(1)}, u32[]{:S(2)}, u32[]{:S(2)}) collective-permute-start(f32[3,18,1,128]{3,2,1,0:T(1,128)S(1)} %get-tuple-element.137), channel_id=1, source_target_pairs={{0,1},{1,2},{2,3},{3,4},{4,5},{5,6},{6,7},{8,9},{9,10},{10,11},{11... | collective-permute-start | bytes 82952 | tf_op jit(solution)/shard_map/ppermute | solution.py:23
  75.4 9.6 %collective-permute-start.20 = (f32[2,2,8,64]{3,2,1,0:T(8,128)S(1)}, f32[2,2,8,64]{3,2,1,0:T(8,128)S(1)}, u32[]{:S(2)}, u32[]{:S(2)}) collective-permute-start(f32[2,2,8,64]{3,2,1,0:T(8,128)S(1)} %get-tuple-element.271), channel_id=1, source_target_pairs={{0,8},{8,16},{16,24},{1,9},{9,17},{17,25},{2,10},{10,18},{18,26},{... | collective-permute-start | bytes 24584 | tf_op jit(solution)/shard_map/ppermute | solution.py:23
  80.1 7.8 %collective-permute-start.8 = (f32[3,1,16,128]{3,2,1,0:T(8,128)S(1)}, f32[3,1,16,128]{3,2,1,0:T(8,128)S(1)}, u32[]{:S(2)}, u32[]{:S(2)}) collective-permute-start(f32[3,1,16,128]{3,2,1,0:T(8,128)S(1)} %get-tuple-element.152), channel_id=1, source_target_pairs={{8,0},{16,8},{24,16},{9,1},{17,9},{25,17},{10,2},{18,10},{26,18},{... | collective-permute-start | bytes 73736 | tf_op jit(solution)/shard_map/ppermute | solution.py:25
  83.1 7.8 %collective-permute-start.9 = (f32[3,1,16,128]{3,2,1,0:T(8,128)S(1)}, f32[3,1,16,128]{3,2,1,0:T(8,128)S(1)}, u32[]{:S(2)}, u32[]{:S(2)}) collective-permute-start(f32[3,1,16,128]{3,2,1,0:T(8,128)S(1)} %get-tuple-element.151), channel_id=1, source_target_pairs={{0,8},{8,16},{16,24},{1,9},{9,17},{17,25},{2,10},{10,18},{18,26},{... | collective-permute-start | bytes 73736 | tf_op jit(solution)/shard_map/ppermute | solution.py:23
  85.1 9.7 %collective-permute-start.23 = (f32[2,12,2,64]{3,2,1,0:T(2,128)S(1)}, f32[2,12,2,64]{3,2,1,0:T(2,128)S(1)}, u32[]{:S(2)}, u32[]{:S(2)}) collective-permute-start(f32[2,12,2,64]{3,2,1,0:T(2,128)S(1)} %get-tuple-element.240), channel_id=1, source_target_pairs={{1,0},{2,1},{3,2},{4,3},{5,4},{6,5},{7,6},{9,8},{10,9},{11,10},{12... | collective-permute-start | bytes 36872 | tf_op jit(solution)/shard_map/ppermute | solution.py:25
  87.9 9.4 %collective-permute-start.22 = (f32[2,12,2,64]{3,2,1,0:T(2,128)S(1)}, f32[2,12,2,64]{3,2,1,0:T(2,128)S(1)}, u32[]{:S(2)}, u32[]{:S(2)}) collective-permute-start(f32[2,12,2,64]{3,2,1,0:T(2,128)S(1)} %get-tuple-element.239), channel_id=1, source_target_pairs={{0,1},{1,2},{2,3},{3,4},{4,5},{5,6},{6,7},{8,9},{9,10},{10,11},{11... | collective-permute-start | bytes 36872 | tf_op jit(solution)/shard_map/ppermute | solution.py:23
  91.0 6.4 %collective-permute-start.10 = (f32[3,18,1,128]{3,2,1,0:T(1,128)S(1)}, f32[3,18,1,128]{3,2,1,0:T(1,128)S(1)}, u32[]{:S(2)}, u32[]{:S(2)}) collective-permute-start(f32[3,18,1,128]{3,2,1,0:T(1,128)S(1)} %get-tuple-element.136), channel_id=1, source_target_pairs={{1,0},{2,1},{3,2},{4,3},{5,4},{6,5},{7,6},{9,8},{10,9},{11,10},{12... | collective-permute-start | bytes 82952 | tf_op jit(solution)/shard_map/ppermute | solution.py:25
  94.7 6.7 %collective-permute-start.11 = (f32[3,18,1,128]{3,2,1,0:T(1,128)S(1)}, f32[3,18,1,128]{3,2,1,0:T(1,128)S(1)}, u32[]{:S(2)}, u32[]{:S(2)}) collective-permute-start(f32[3,18,1,128]{3,2,1,0:T(1,128)S(1)} %get-tuple-element.135), channel_id=1, source_target_pairs={{0,1},{1,2},{2,3},{3,4},{4,5},{5,6},{6,7},{8,9},{9,10},{10,11},{11... | collective-permute-start | bytes 82952 | tf_op jit(solution)/shard_map/ppermute | solution.py:23
  111.0 6.0 %collective-permute-start.14 = (f32[3,18,1,128]{3,2,1,0:T(1,128)S(1)}, f32[3,18,1,128]{3,2,1,0:T(1,128)S(1)}, u32[]{:S(2)}, u32[]{:S(2)}) collective-permute-start(f32[3,18,1,128]{3,2,1,0:T(1,128)S(1)} %get-tuple-element.134), channel_id=1, source_target_pairs={{1,0},{2,1},{3,2},{4,3},{5,4},{6,5},{7,6},{9,8},{10,9},{11,10},{12... | collective-permute-start | bytes 82952 | tf_op jit(solution)/shard_map/ppermute | solution.py:25
  112.9 6.7 %collective-permute-start.15 = (f32[3,18,1,128]{3,2,1,0:T(1,128)S(1)}, f32[3,18,1,128]{3,2,1,0:T(1,128)S(1)}, u32[]{:S(2)}, u32[]{:S(2)}) collective-permute-start(f32[3,18,1,128]{3,2,1,0:T(1,128)S(1)} %get-tuple-element.133), channel_id=1, source_target_pairs={{0,1},{1,2},{2,3},{3,4},{4,5},{5,6},{6,7},{8,9},{9,10},{10,11},{11... | collective-permute-start | bytes 82952 | tf_op jit(solution)/shard_map/ppermute | solution.py:23
  129.0 5.9 %collective-permute-start.18 = (f32[3,18,1,128]{3,2,1,0:T(1,128)S(1)}, f32[3,18,1,128]{3,2,1,0:T(1,128)S(1)}, u32[]{:S(2)}, u32[]{:S(2)}) collective-permute-start(f32[3,18,1,128]{3,2,1,0:T(1,128)S(1)} %get-tuple-element.132), channel_id=1, source_target_pairs={{1,0},{2,1},{3,2},{4,3},{5,4},{6,5},{7,6},{9,8},{10,9},{11,10},{12... | collective-permute-start | bytes 82952 | tf_op jit(solution)/shard_map/ppermute | solution.py:25
  131.9 6.7 %collective-permute-start.19 = (f32[3,18,1,128]{3,2,1,0:T(1,128)S(1)}, f32[3,18,1,128]{3,2,1,0:T(1,128)S(1)}, u32[]{:S(2)}, u32[]{:S(2)}) collective-permute-start(f32[3,18,1,128]{3,2,1,0:T(1,128)S(1)} %get-tuple-element.131), channel_id=1, source_target_pairs={{0,1},{1,2},{2,3},{3,4},{4,5},{5,6},{6,7},{8,9},{9,10},{10,11},{11... | collective-permute-start | bytes 82952 | tf_op jit(solution)/shard_map/ppermute | solution.py:23
  183.6 6.7 %collective-permute-start.26 = (f32[3,10,1,64]{3,2,1,0:T(1,128)S(1)}, f32[3,10,1,64]{3,2,1,0:T(1,128)S(1)}, u32[]{:S(2)}, u32[]{:S(2)}) collective-permute-start(f32[3,10,1,64]{3,2,1,0:T(1,128)S(1)} %get-tuple-element.220), channel_id=1, source_target_pairs={{1,0},{2,1},{3,2},{4,3},{5,4},{6,5},{7,6},{9,8},{10,9},{11,10},{12... | collective-permute-start | bytes 23048 | tf_op jit(solution)/shard_map/ppermute | solution.py:25
  185.5 6.5 %collective-permute-start.27 = (f32[3,10,1,64]{3,2,1,0:T(1,128)S(1)}, f32[3,10,1,64]{3,2,1,0:T(1,128)S(1)}, u32[]{:S(2)}, u32[]{:S(2)}) collective-permute-start(f32[3,10,1,64]{3,2,1,0:T(1,128)S(1)} %get-tuple-element.219), channel_id=1, source_target_pairs={{0,1},{1,2},{2,3},{3,4},{4,5},{5,6},{6,7},{8,9},{9,10},{10,11},{11... | collective-permute-start | bytes 23048 | tf_op jit(solution)/shard_map/ppermute | solution.py:23
  192.8 7.3 %collective-permute-start.28 = (f32[3,1,8,64]{3,2,1,0:T(8,128)S(1)}, f32[3,1,8,64]{3,2,1,0:T(8,128)S(1)}, u32[]{:S(2)}, u32[]{:S(2)}) collective-permute-start(f32[3,1,8,64]{3,2,1,0:T(8,128)S(1)} %get-tuple-element.236), channel_id=1, source_target_pairs={{8,0},{16,8},{24,16},{9,1},{17,9},{25,17},{10,2},{18,10},{26,18},{... | collective-permute-start | bytes 18440 | tf_op jit(solution)/shard_map/ppermute | solution.py:25
  194.7 8.3 %collective-permute-start.29 = (f32[3,1,8,64]{3,2,1,0:T(8,128)S(1)}, f32[3,1,8,64]{3,2,1,0:T(8,128)S(1)}, u32[]{:S(2)}, u32[]{:S(2)}) collective-permute-start(f32[3,1,8,64]{3,2,1,0:T(8,128)S(1)} %get-tuple-element.235), channel_id=1, source_target_pairs={{0,8},{8,16},{16,24},{1,9},{9,17},{17,25},{2,10},{10,18},{18,26},{... | collective-permute-start | bytes 18440 | tf_op jit(solution)/shard_map/ppermute | solution.py:23
  197.1 9.7 %collective-permute-start.43 = (f32[2,8,2,32]{3,2,1,0:T(2,128)S(1)}, f32[2,8,2,32]{3,2,1,0:T(2,128)S(1)}, u32[]{:S(2)}, u32[]{:S(2)}) collective-permute-start(f32[2,8,2,32]{3,2,1,0:T(2,128)S(1)} %get-tuple-element.296), channel_id=1, source_target_pairs={{1,0},{2,1},{3,2},{4,3},{5,4},{6,5},{7,6},{9,8},{10,9},{11,10},{12... | collective-permute-start | bytes 12296 | tf_op jit(solution)/shard_map/ppermute | solution.py:25
  200.1 8.8 %collective-permute-start.42 = (f32[2,8,2,32]{3,2,1,0:T(2,128)S(1)}, f32[2,8,2,32]{3,2,1,0:T(2,128)S(1)}, u32[]{:S(2)}, u32[]{:S(2)}) collective-permute-start(f32[2,8,2,32]{3,2,1,0:T(2,128)S(1)} %get-tuple-element.295), channel_id=1, source_target_pairs={{0,1},{1,2},{2,3},{3,4},{4,5},{5,6},{6,7},{8,9},{9,10},{10,11},{11... | collective-permute-start | bytes 12296 | tf_op jit(solution)/shard_map/ppermute | solution.py:23
  203.1 5.9 %collective-permute-start.30 = (f32[3,10,1,64]{3,2,1,0:T(1,128)S(1)}, f32[3,10,1,64]{3,2,1,0:T(1,128)S(1)}, u32[]{:S(2)}, u32[]{:S(2)}) collective-permute-start(f32[3,10,1,64]{3,2,1,0:T(1,128)S(1)} %get-tuple-element.218), channel_id=1, source_target_pairs={{1,0},{2,1},{3,2},{4,3},{5,4},{6,5},{7,6},{9,8},{10,9},{11,10},{12... | collective-permute-start | bytes 23048 | tf_op jit(solution)/shard_map/ppermute | solution.py:25
  206.9 6.5 %collective-permute-start.31 = (f32[3,10,1,64]{3,2,1,0:T(1,128)S(1)}, f32[3,10,1,64]{3,2,1,0:T(1,128)S(1)}, u32[]{:S(2)}, u32[]{:S(2)}) collective-permute-start(f32[3,10,1,64]{3,2,1,0:T(1,128)S(1)} %get-tuple-element.217), channel_id=1, source_target_pairs={{0,1},{1,2},{2,3},{3,4},{4,5},{5,6},{6,7},{8,9},{9,10},{10,11},{11... | collective-permute-start | bytes 23048 | tf_op jit(solution)/shard_map/ppermute | solution.py:23
  221.1 6.0 %collective-permute-start.34 = (f32[3,10,1,64]{3,2,1,0:T(1,128)S(1)}, f32[3,10,1,64]{3,2,1,0:T(1,128)S(1)}, u32[]{:S(2)}, u32[]{:S(2)}) collective-permute-start(f32[3,10,1,64]{3,2,1,0:T(1,128)S(1)} %get-tuple-element.216), channel_id=1, source_target_pairs={{1,0},{2,1},{3,2},{4,3},{5,4},{6,5},{7,6},{9,8},{10,9},{11,10},{12... | collective-permute-start | bytes 23048 | tf_op jit(solution)/shard_map/ppermute | solution.py:25
  223.1 6.5 %collective-permute-start.35 = (f32[3,10,1,64]{3,2,1,0:T(1,128)S(1)}, f32[3,10,1,64]{3,2,1,0:T(1,128)S(1)}, u32[]{:S(2)}, u32[]{:S(2)}) collective-permute-start(f32[3,10,1,64]{3,2,1,0:T(1,128)S(1)} %get-tuple-element.215), channel_id=1, source_target_pairs={{0,1},{1,2},{2,3},{3,4},{4,5},{5,6},{6,7},{8,9},{9,10},{10,11},{11... | collective-permute-start | bytes 23048 | tf_op jit(solution)/shard_map/ppermute | solution.py:23
  237.4 10.8 %collective-permute-start.38 = (f32[3,10,1,64]{3,2,1,0:T(1,128)S(1)}, f32[3,10,1,64]{3,2,1,0:T(1,128)S(1)}, u32[]{:S(2)}, u32[]{:S(2)}) collective-permute-start(f32[3,10,1,64]{3,2,1,0:T(1,128)S(1)} %get-tuple-element.214), channel_id=1, source_target_pairs={{1,0},{2,1},{3,2},{4,3},{5,4},{6,5},{7,6},{9,8},{10,9},{11,10},{12... | collective-permute-start | bytes 23048 | tf_op jit(solution)/shard_map/ppermute | solution.py:25
  239.4 8.9 %collective-permute-start.39 = (f32[3,10,1,64]{3,2,1,0:T(1,128)S(1)}, f32[3,10,1,64]{3,2,1,0:T(1,128)S(1)}, u32[]{:S(2)}, u32[]{:S(2)}) collective-permute-start(f32[3,10,1,64]{3,2,1,0:T(1,128)S(1)} %get-tuple-element.213), channel_id=1, source_target_pairs={{0,1},{1,2},{2,3},{3,4},{4,5},{5,6},{6,7},{8,9},{9,10},{10,11},{11... | collective-permute-start | bytes 23048 | tf_op jit(solution)/shard_map/ppermute | solution.py:23
  266.9 6.6 %collective-permute-start.46 = (f32[3,6,1,32]{3,2,1,0:T(1,128)S(1)}, f32[3,6,1,32]{3,2,1,0:T(1,128)S(1)}, u32[]{:S(2)}, u32[]{:S(2)}) collective-permute-start(f32[3,6,1,32]{3,2,1,0:T(1,128)S(1)} %get-tuple-element.294), channel_id=1, source_target_pairs={{1,0},{2,1},{3,2},{4,3},{5,4},{6,5},{7,6},{9,8},{10,9},{11,10},{12... | collective-permute-start | bytes 6920 | tf_op jit(solution)/shard_map/ppermute | solution.py:25
  269.8 6.5 %collective-permute-start.47 = (f32[3,6,1,32]{3,2,1,0:T(1,128)S(1)}, f32[3,6,1,32]{3,2,1,0:T(1,128)S(1)}, u32[]{:S(2)}, u32[]{:S(2)}) collective-permute-start(f32[3,6,1,32]{3,2,1,0:T(1,128)S(1)} %get-tuple-element.293), channel_id=1, source_target_pairs={{0,1},{1,2},{2,3},{3,4},{4,5},{5,6},{6,7},{8,9},{9,10},{10,11},{11... | collective-permute-start | bytes 6920 | tf_op jit(solution)/shard_map/ppermute | solution.py:23
  276.7 10.9 %collective-permute-start.48 = (f32[3,1,4,32]{3,2,1,0:T(4,128)S(1)}, f32[3,1,4,32]{3,2,1,0:T(4,128)S(1)}, u32[]{:S(2)}, u32[]{:S(2)}) collective-permute-start(f32[3,1,4,32]{3,2,1,0:T(4,128)S(1)} %get-tuple-element.320), channel_id=1, source_target_pairs={{8,0},{16,8},{24,16},{9,1},{17,9},{25,17},{10,2},{18,10},{26,18},{... | collective-permute-start | bytes 4616 | tf_op jit(solution)/shard_map/ppermute | solution.py:25
  278.7 9.0 %collective-permute-start.49 = (f32[3,1,4,32]{3,2,1,0:T(4,128)S(1)}, f32[3,1,4,32]{3,2,1,0:T(4,128)S(1)}, u32[]{:S(2)}, u32[]{:S(2)}) collective-permute-start(f32[3,1,4,32]{3,2,1,0:T(4,128)S(1)} %get-tuple-element.319), channel_id=1, source_target_pairs={{0,8},{8,16},{16,24},{1,9},{9,17},{17,25},{2,10},{10,18},{18,26},{... | collective-permute-start | bytes 4616 | tf_op jit(solution)/shard_map/ppermute | solution.py:23
  281.8 11.7 %collective-permute-start.63 = (f32[2,6,2,16]{3,2,1,0:T(2,128)S(1)}, f32[2,6,2,16]{3,2,1,0:T(2,128)S(1)}, u32[]{:S(2)}, u32[]{:S(2)}) collective-permute-start(f32[2,6,2,16]{3,2,1,0:T(2,128)S(1)} %pad_maximum_fusion.254), channel_id=1, source_target_pairs={{1,0},{2,1},{3,2},{4,3},{5,4},{6,5},{7,6},{9,8},{10,9},{11,10},{12... | collective-permute-start | bytes 4616 | tf_op jit(solution)/shard_map/ppermute | solution.py:25
  283.7 9.8 %collective-permute-start.62 = (f32[2,6,2,16]{3,2,1,0:T(2,128)S(1)}, f32[2,6,2,16]{3,2,1,0:T(2,128)S(1)}, u32[]{:S(2)}, u32[]{:S(2)}) collective-permute-start(f32[2,6,2,16]{3,2,1,0:T(2,128)S(1)} %pad_maximum_fusion.254), channel_id=1, source_target_pairs={{0,1},{1,2},{2,3},{3,4},{4,5},{5,6},{6,7},{8,9},{9,10},{10,11},{11... | collective-permute-start | bytes 4616 | tf_op jit(solution)/shard_map/ppermute | solution.py:23
  287.7 6.6 %collective-permute-start.50 = (f32[3,6,1,32]{3,2,1,0:T(1,128)S(1)}, f32[3,6,1,32]{3,2,1,0:T(1,128)S(1)}, u32[]{:S(2)}, u32[]{:S(2)}) collective-permute-start(f32[3,6,1,32]{3,2,1,0:T(1,128)S(1)} %get-tuple-element.292), channel_id=1, source_target_pairs={{1,0},{2,1},{3,2},{4,3},{5,4},{6,5},{7,6},{9,8},{10,9},{11,10},{12... | collective-permute-start | bytes 6920 | tf_op jit(solution)/shard_map/ppermute | solution.py:25
  290.5 6.5 %collective-permute-start.51 = (f32[3,6,1,32]{3,2,1,0:T(1,128)S(1)}, f32[3,6,1,32]{3,2,1,0:T(1,128)S(1)}, u32[]{:S(2)}, u32[]{:S(2)}) collective-permute-start(f32[3,6,1,32]{3,2,1,0:T(1,128)S(1)} %get-tuple-element.291), channel_id=1, source_target_pairs={{0,1},{1,2},{2,3},{3,4},{4,5},{5,6},{6,7},{8,9},{9,10},{10,11},{11... | collective-permute-start | bytes 6920 | tf_op jit(solution)/shard_map/ppermute | solution.py:23
  304.4 6.6 %collective-permute-start.54 = (f32[3,6,1,32]{3,2,1,0:T(1,128)S(1)}, f32[3,6,1,32]{3,2,1,0:T(1,128)S(1)}, u32[]{:S(2)}, u32[]{:S(2)}) collective-permute-start(f32[3,6,1,32]{3,2,1,0:T(1,128)S(1)} %get-tuple-element.290), channel_id=1, source_target_pairs={{1,0},{2,1},{3,2},{4,3},{5,4},{6,5},{7,6},{9,8},{10,9},{11,10},{12... | collective-permute-start | bytes 6920 | tf_op jit(solution)/shard_map/ppermute | solution.py:25
  306.3 6.5 %collective-permute-start.55 = (f32[3,6,1,32]{3,2,1,0:T(1,128)S(1)}, f32[3,6,1,32]{3,2,1,0:T(1,128)S(1)}, u32[]{:S(2)}, u32[]{:S(2)}) collective-permute-start(f32[3,6,1,32]{3,2,1,0:T(1,128)S(1)} %get-tuple-element.289), channel_id=1, source_target_pairs={{0,1},{1,2},{2,3},{3,4},{4,5},{5,6},{6,7},{8,9},{9,10},{10,11},{11... | collective-permute-start | bytes 6920 | tf_op jit(solution)/shard_map/ppermute | solution.py:23
  320.2 6.8 %collective-permute-start.58 = (f32[3,6,1,32]{3,2,1,0:T(1,128)S(1)}, f32[3,6,1,32]{3,2,1,0:T(1,128)S(1)}, u32[]{:S(2)}, u32[]{:S(2)}) collective-permute-start(f32[3,6,1,32]{3,2,1,0:T(1,128)S(1)} %get-tuple-element.288), channel_id=1, source_target_pairs={{1,0},{2,1},{3,2},{4,3},{5,4},{6,5},{7,6},{9,8},{10,9},{11,10},{12... | collective-permute-start | bytes 6920 | tf_op jit(solution)/shard_map/ppermute | solution.py:25
  322.1 6.5 %collective-permute-start.59 = (f32[3,6,1,32]{3,2,1,0:T(1,128)S(1)}, f32[3,6,1,32]{3,2,1,0:T(1,128)S(1)}, u32[]{:S(2)}, u32[]{:S(2)}) collective-permute-start(f32[3,6,1,32]{3,2,1,0:T(1,128)S(1)} %get-tuple-element.287), channel_id=1, source_target_pairs={{0,1},{1,2},{2,3},{3,4},{4,5},{5,6},{6,7},{8,9},{9,10},{10,11},{11... | collective-permute-start | bytes 6920 | tf_op jit(solution)/shard_map/ppermute | solution.py:23
  336.4 5.9 collective-permute-start.66
  338.3 6.4 %collective-permute-start.67 = (f32[3,4,1,16]{3,2,1,0:T(1,128)S(1)}, f32[3,4,1,16]{3,2,1,0:T(1,128)S(1)}, u32[]{:S(2)}, u32[]{:S(2)}) collective-permute-start(f32[3,4,1,16]{3,2,1,0:T(1,128)S(1)} %get-tuple-element.335), channel_id=1, source_target_pairs={{0,1},{1,2},{2,3},{3,4},{4,5},{5,6},{6,7},{8,9},{9,10},{10,11},{11... | collective-permute-start | bytes 2312 | tf_op jit(solution)/shard_map/ppermute | solution.py:23
  354.0 6.4 %collective-permute-start.71 = (f32[3,4,1,16]{3,2,1,0:T(1,128)S(1)}, f32[3,4,1,16]{3,2,1,0:T(1,128)S(1)}, u32[]{:S(2)}, u32[]{:S(2)}) collective-permute-start(f32[3,4,1,16]{3,2,1,0:T(1,128)S(1)} %get-tuple-element.333), channel_id=1, source_target_pairs={{0,1},{1,2},{2,3},{3,4},{4,5},{5,6},{6,7},{8,9},{9,10},{10,11},{11... | collective-permute-start | bytes 2312 | tf_op jit(solution)/shard_map/ppermute | solution.py:23
  369.7 6.4 %collective-permute-start.75 = (f32[3,4,1,16]{3,2,1,0:T(1,128)S(1)}, f32[3,4,1,16]{3,2,1,0:T(1,128)S(1)}, u32[]{:S(2)}, u32[]{:S(2)}) collective-permute-start(f32[3,4,1,16]{3,2,1,0:T(1,128)S(1)} %get-tuple-element.331), channel_id=1, source_target_pairs={{0,1},{1,2},{2,3},{3,4},{4,5},{5,6},{6,7},{8,9},{9,10},{10,11},{11... | collective-permute-start | bytes 2312 | tf_op jit(solution)/shard_map/ppermute | solution.py:23
  385.8 6.5 %collective-permute-start.79 = (f32[3,6,1,32]{3,2,1,0:T(1,128)S(1)}, f32[3,6,1,32]{3,2,1,0:T(1,128)S(1)}, u32[]{:S(2)}, u32[]{:S(2)}) collective-permute-start(f32[3,6,1,32]{3,2,1,0:T(1,128)S(1)} %get-tuple-element.285), channel_id=1, source_target_pairs={{0,1},{1,2},{2,3},{3,4},{4,5},{5,6},{6,7},{8,9},{9,10},{10,11},{11... | collective-permute-start | bytes 6920 | tf_op jit(solution)/shard_map/ppermute | solution.py:23
  401.6 6.5 %collective-permute-start.83 = (f32[3,6,1,32]{3,2,1,0:T(1,128)S(1)}, f32[3,6,1,32]{3,2,1,0:T(1,128)S(1)}, u32[]{:S(2)}, u32[]{:S(2)}) collective-permute-start(f32[3,6,1,32]{3,2,1,0:T(1,128)S(1)} %get-tuple-element.283), channel_id=1, source_target_pairs={{0,1},{1,2},{2,3},{3,4},{4,5},{5,6},{6,7},{8,9},{9,10},{10,11},{11... | collective-permute-start | bytes 6920 | tf_op jit(solution)/shard_map/ppermute | solution.py:23
  417.4 6.5 %collective-permute-start.87 = (f32[3,6,1,32]{3,2,1,0:T(1,128)S(1)}, f32[3,6,1,32]{3,2,1,0:T(1,128)S(1)}, u32[]{:S(2)}, u32[]{:S(2)}) collective-permute-start(f32[3,6,1,32]{3,2,1,0:T(1,128)S(1)} %get-tuple-element.281), channel_id=1, source_target_pairs={{0,1},{1,2},{2,3},{3,4},{4,5},{5,6},{6,7},{8,9},{9,10},{10,11},{11... | collective-permute-start | bytes 6920 | tf_op jit(solution)/shard_map/ppermute | solution.py:23
  431.3 6.1 %collective-permute-start.90 = (f32[3,6,1,32]{3,2,1,0:T(1,128)S(1)}, f32[3,6,1,32]{3,2,1,0:T(1,128)S(1)}, u32[]{:S(2)}, u32[]{:S(2)}) collective-permute-start(f32[3,6,1,32]{3,2,1,0:T(1,128)S(1)} %get-tuple-element.280), channel_id=1, source_target_pairs={{1,0},{2,1},{3,2},{4,3},{5,4},{6,5},{7,6},{9,8},{10,9},{11,10},{12... | collective-permute-start | bytes 6920 | tf_op jit(solution)/shard_map/ppermute | solution.py:25
  433.2 6.5 %collective-permute-start.91 = (f32[3,6,1,32]{3,2,1,0:T(1,128)S(1)}, f32[3,6,1,32]{3,2,1,0:T(1,128)S(1)}, u32[]{:S(2)}, u32[]{:S(2)}) collective-permute-start(f32[3,6,1,32]{3,2,1,0:T(1,128)S(1)} %get-tuple-element.279), channel_id=1, source_target_pairs={{0,1},{1,2},{2,3},{3,4},{4,5},{5,6},{6,7},{8,9},{9,10},{10,11},{11... | collective-permute-start | bytes 6920 | tf_op jit(solution)/shard_map/ppermute | solution.py:23
  452.4 6.5 %collective-permute-start.95 = (f32[3,10,1,64]{3,2,1,0:T(1,128)S(1)}, f32[3,10,1,64]{3,2,1,0:T(1,128)S(1)}, u32[]{:S(2)}, u32[]{:S(2)}) collective-permute-start(f32[3,10,1,64]{3,2,1,0:T(1,128)S(1)} %get-tuple-element.211), channel_id=1, source_target_pairs={{0,1},{1,2},{2,3},{3,4},{4,5},{5,6},{6,7},{8,9},{9,10},{10,11},{11... | collective-permute-start | bytes 23048 | tf_op jit(solution)/shard_map/ppermute | solution.py:23
  468.5 6.5 %collective-permute-start.99 = (f32[3,10,1,64]{3,2,1,0:T(1,128)S(1)}, f32[3,10,1,64]{3,2,1,0:T(1,128)S(1)}, u32[]{:S(2)}, u32[]{:S(2)}) collective-permute-start(f32[3,10,1,64]{3,2,1,0:T(1,128)S(1)} %get-tuple-element.209), channel_id=1, source_target_pairs={{0,1},{1,2},{2,3},{3,4},{4,5},{5,6},{6,7},{8,9},{9,10},{10,11},{11... | collective-permute-start | bytes 23048 | tf_op jit(solution)/shard_map/ppermute | solution.py:23
  484.7 6.5 %collective-permute-start.103 = (f32[3,10,1,64]{3,2,1,0:T(1,128)S(1)}, f32[3,10,1,64]{3,2,1,0:T(1,128)S(1)}, u32[]{:S(2)}, u32[]{:S(2)}) collective-permute-start(f32[3,10,1,64]{3,2,1,0:T(1,128)S(1)} %get-tuple-element.207), channel_id=1, source_target_pairs={{0,1},{1,2},{2,3},{3,4},{4,5},{5,6},{6,7},{8,9},{9,10},{10,11},{11... | collective-permute-start | bytes 23048 | tf_op jit(solution)/shard_map/ppermute | solution.py:23
  500.9 6.5 %collective-permute-start.107 = (f32[3,10,1,64]{3,2,1,0:T(1,128)S(1)}, f32[3,10,1,64]{3,2,1,0:T(1,128)S(1)}, u32[]{:S(2)}, u32[]{:S(2)}) collective-permute-start(f32[3,10,1,64]{3,2,1,0:T(1,128)S(1)} %get-tuple-element.205), channel_id=1, source_target_pairs={{0,1},{1,2},{2,3},{3,4},{4,5},{5,6},{6,7},{8,9},{9,10},{10,11},{11... | collective-permute-start | bytes 23048 | tf_op jit(solution)/shard_map/ppermute | solution.py:23
  522.6 5.9 collective-permute-start.110
  524.5 6.7 %collective-permute-start.111 = (f32[3,18,1,128]{3,2,1,0:T(1,128)S(1)}, f32[3,18,1,128]{3,2,1,0:T(1,128)S(1)}, u32[]{:S(2)}, u32[]{:S(2)}) collective-permute-start(f32[3,18,1,128]{3,2,1,0:T(1,128)S(1)} %get-tuple-element.129), channel_id=1, source_target_pairs={{0,1},{1,2},{2,3},{3,4},{4,5},{5,6},{6,7},{8,9},{9,10},{10,11},{11... | collective-permute-start | bytes 82952 | tf_op jit(solution)/shard_map/ppermute | solution.py:23
  540.4 5.9 collective-permute-start.114
  542.3 6.7 %collective-permute-start.115 = (f32[3,18,1,128]{3,2,1,0:T(1,128)S(1)}, f32[3,18,1,128]{3,2,1,0:T(1,128)S(1)}, u32[]{:S(2)}, u32[]{:S(2)}) collective-permute-start(f32[3,18,1,128]{3,2,1,0:T(1,128)S(1)} %get-tuple-element.127), channel_id=1, source_target_pairs={{0,1},{1,2},{2,3},{3,4},{4,5},{5,6},{6,7},{8,9},{9,10},{10,11},{11... | collective-permute-start | bytes 82952 | tf_op jit(solution)/shard_map/ppermute | solution.py:23
  558.2 6.1 %collective-permute-start.118 = (f32[3,18,1,128]{3,2,1,0:T(1,128)S(1)}, f32[3,18,1,128]{3,2,1,0:T(1,128)S(1)}, u32[]{:S(2)}, u32[]{:S(2)}) collective-permute-start(f32[3,18,1,128]{3,2,1,0:T(1,128)S(1)} %get-tuple-element.126), channel_id=1, source_target_pairs={{1,0},{2,1},{3,2},{4,3},{5,4},{6,5},{7,6},{9,8},{10,9},{11,10},{12... | collective-permute-start | bytes 82952 | tf_op jit(solution)/shard_map/ppermute | solution.py:25
  560.1 6.7 %collective-permute-start.119 = (f32[3,18,1,128]{3,2,1,0:T(1,128)S(1)}, f32[3,18,1,128]{3,2,1,0:T(1,128)S(1)}, u32[]{:S(2)}, u32[]{:S(2)}) collective-permute-start(f32[3,18,1,128]{3,2,1,0:T(1,128)S(1)} %get-tuple-element.125), channel_id=1, source_target_pairs={{0,1},{1,2},{2,3},{3,4},{4,5},{5,6},{6,7},{8,9},{9,10},{10,11},{11... | collective-permute-start | bytes 82952 | tf_op jit(solution)/shard_map/ppermute | solution.py:23
  578.1 6.7 %collective-permute-start.123 = (f32[3,18,1,128]{3,2,1,0:T(1,128)S(1)}, f32[3,18,1,128]{3,2,1,0:T(1,128)S(1)}, u32[]{:S(2)}, u32[]{:S(2)}) collective-permute-start(f32[3,18,1,128]{3,2,1,0:T(1,128)S(1)} %get-tuple-element.123), channel_id=1, source_target_pairs={{0,1},{1,2},{2,3},{3,4},{4,5},{5,6},{6,7},{8,9},{9,10},{10,11},{11... | collective-permute-start | bytes 82952 | tf_op jit(solution)/shard_map/ppermute | solution.py:23
  (97 other events, 776.8 us)
where the time goes:
time: 599 us; the launch traced here: 588 us
  starting transfers between devices  319 us (53%)
  waiting for transfers between devices  132 us (22%)
  local copies, waits for them, and re-layouts  76.7 us (13%)
  other arithmetic  56.3 us (9%)
    ppermute x62, starting transfers between devices, with_halo(): lax.ppermute(tail, axis, [(i, (i + 1) % count) for i in range(ends)])  186 us
    ppermute x62, starting transfers between devices, with_halo(): lax.ppermute(head, axis, [((i + 1) % count, i) for i in range(ends)])  133 us
    ppermute x62, waiting for transfers between devices, with_halo(): lax.ppermute(tail, axis, [(i, (i + 1) % count) for i in range(ends)])  132 us
    reshape x1, local copies, waits for them, and re-layouts, shrink(): blocks = array.reshape(comps, rows // 2, 2, cols // 2, 2, depth // 2, 2)  26.5 us
    reduce_sum x6, other arithmetic, shrink(): return blocks.mean(axis=(2, 4, 6))  22 us
    another operation x2, local copies, waits for them, and re-layouts, on_device(): coeff = jnp.stack([stiffness, reaction])  20.2 us
  transfers between devices with their start and end apart: 124, of which 51 were waited for; matrix products, arithmetic and copies ran while one was open for 12% of the time, Pallas kernels for 0%

commit v1 on v0

v1 whole, which is shorter than its diff:
```python
import jax
import jax.numpy as jnp
from jax import lax
from jax.experimental import pallas as pl
from jax.experimental.pallas import tpu as pltpu
from jax.sharding import PartitionSpec as P

BETA = 1.0
THETA = 1.5
DELTA = 1.0
SIGMA = 1.5
HX = 6
HY = 8
LANES = 128
DIRS = [(a, b) for a in (-1, 0, 1) for b in (-1, 0, 1) if (a, b) != (0, 0)]


def rate_list():
    rates = [1.0 / SIGMA]
    for number in range(3):
        rates.append(1.0 / (2.0 * SIGMA - rates[-1]))
    return rates


def round8(number):
    return -(-number // 8) * 8


def lane(rows):
    return lax.broadcasted_iota(jnp.int32, (rows, LANES), 1)


def roll(value, shift):
    return pltpu.roll(value, shift % LANES, 1)


def pack(values, group):
    if group == 1:
        return values[0]
    place = lane(values[0].shape[0]) % group
    out = values[0]
    for t in range(1, len(values)):
        out = jnp.where(place == t, values[t], out)
    return out


def unpack(value, group, t):
    if group == 1:
        return value
    out = jnp.where(lane(value.shape[0]) % group == t, value, 0.0)
    if t:
        out = roll(out, -t)
    shift = 1
    while shift < group:
        out = out + roll(out, shift)
        shift *= 2
    return out


def halve_lanes(value, group):
    first = lane(value.shape[0]) % (2 * group) < group
    return value + jnp.where(first, roll(value, -group), roll(value, group))


class Exchange:
    def __init__(self, size, group, packed, widths):
        self.size, self.group, self.packed, self.widths = size, group, packed, widths
        self.blocks = size // group
        self.offs = [sum(widths[:n]) for n in range(len(widths))]
        self.rows = round8(sum(widths))
        self.xrows = round8(len(widths) * size)

    def scratch(self):
        f32 = jnp.float32
        return [
            pltpu.VMEM((2, self.packed, self.xrows, LANES), f32),
            pltpu.VMEM((2, self.blocks, self.rows, LANES), f32),
            pltpu.VMEM((2, self.packed, self.xrows, LANES), f32),
            pltpu.VMEM((2, self.blocks + 2 * self.packed, self.rows, LANES), f32),
            pltpu.SemaphoreType.DMA((8,)),
            pltpu.SemaphoreType.DMA((8,)),
        ]

    def bind(self, refs, where):
        self.sx, self.sy, self.rx, self.ry, self.ssem, self.rsem = refs
        self.where = where

    def copy(self, ex, ey):
        g, b, _ = self.where
        n, w = self.blocks, self.packed
        if ey == 0:
            side = 0 if ex < 0 else 1
            src, dst = self.sx.at[side], self.rx.at[1 - side]
        else:
            side = 0 if ey < 0 else 1
            src, dst = self.sy.at[side], self.ry.at[1 - side]
            if ex == 0:
                dst = dst.at[pl.ds(w, n)]
            elif ex < 0:
                src, dst = src.at[pl.ds(0, w)], dst.at[pl.ds(w + n, w)]
            else:
                src, dst = src.at[pl.ds(n - w, w)], dst.at[pl.ds(0, w)]
        return pltpu.make_async_remote_copy(
            src_ref=src,
            dst_ref=dst,
            send_sem=self.ssem.at[DIRS.index((ex, ey))],
            recv_sem=self.rsem.at[DIRS.index((-ex, -ey))],
            device_id=(g + ex, b + ey),
            device_id_type=pl.DeviceIdType.MESH,
        )

    def stage(self, get):
        def put(j, field, r0, count, ref, side, row, off):
            values = [get(field, j * self.group + t, r0, count) for t in range(self.group)]
            ref[side, row, off : off + count, :] = pack(values, self.group)

        def body(j, carry):
            for field, width in enumerate(self.widths):
                for side in (0, 1):
                    r0 = 0 if side == 0 else self.size - width
                    put(j, field, r0, width, self.sy, side, j, self.offs[field])
            return carry

        if self.blocks > 4:
            lax.fori_loop(0, self.blocks, body, 0)
        else:
            for j in range(self.blocks):
                body(j, 0)
        for side in (0, 1):
            for j in range(self.packed):
                for field in range(len(self.widths)):
                    at = j if side == 0 else self.blocks - self.packed + j
                    put(at, field, 0, self.size, self.sx, side, j, field * self.size)

    def start(self):
        exists = self.where[2]
        for d in DIRS:
            @pl.when(exists[d])
            def _(d=d):
                self.copy(*d).start()

    def finish_send(self):
        exists = self.where[2]
        for d in DIRS:
            @pl.when(exists[d])
            def _(d=d):
                self.copy(*d).wait_send()

    def finish(self, put):
        exists = self.where[2]
        size, group = self.size, self.group

        def spread_rows(ref, side, row, x0, off, field, y0, count):
            value = ref[side, row, off : off + count, :]
            for t in range(group):
                put(field, x0 + t, y0, unpack(value, group, t))

        for d in DIRS:
            @pl.when(exists[d])
            def _(d=d):
                dx, dy = d
                self.copy(-dx, -dy).wait_recv()
                if dy == 0:
                    side = 0 if dx < 0 else 1
                    base = -self.packed * group if dx < 0 else size
                    for j in range(self.packed):
                        for field in range(len(self.widths)):
                            spread_rows(
                                self.rx, side, j, base + j * group, field * size, field, 0, size
                            )
                    return
                side = 0 if dy < 0 else 1
                first, count = {
                    -1: (0, self.packed),
                    0: (self.packed, self.blocks),
                    1: (self.packed + self.blocks, self.packed),
                }[dx]

                def body(j, carry):
                    for field, width in enumerate(self.widths):
                        y0 = -width if dy < 0 else size
                        spread_rows(
                            self.ry,
                            side,
                            first + j,
                            (first + j - self.packed) * group,
                            self.offs[field],
                            field,
                            y0,
                            width,
                        )
                    return carry

                if count > 4:
                    lax.fori_loop(0, count, body, 0)
                else:
                    for j in range(count):
                        body(j, 0)


class Level:
    NAMES = ("f", "xa", "xb", "p")
    COEFF = ("k", "rea", "kx", "ky", "kz", "kzm", "dg", "inv")

    def __init__(self, number, xsize, ysize, window):
        self.number, self.xsize, self.ysize, self.window = number, xsize, ysize, window
        self.group = 2**number
        self.scale = 0.25**number
        self.shape = (xsize + 2 * HX, round8(ysize) + 2 * HY, LANES)

    def scratch(self):
        f32 = jnp.float32
        return [pltpu.VMEM((3,) + self.shape, f32) for _ in self.NAMES] + [
            pltpu.VMEM(self.shape, f32) for _ in self.COEFF
        ]

    def bind(self, refs):
        for name, ref in zip(self.NAMES + self.COEFF, refs):
            setattr(self, name, ref)

    def clear(self):
        zero = jnp.zeros(self.shape[1:], jnp.float32)

        def body(i, carry):
            for name in self.NAMES:
                for c in range(3):
                    getattr(self, name)[c, i] = zero
            for name in self.COEFF:
                getattr(self, name)[i] = zero
            return carry

        lax.fori_loop(0, self.shape[0], body, 0)

    def prepare(self, halo, gx0, gy0, xcount, ycount):
        w0, wn = self.window
        z = self.group
        s = self.scale
        lanes = lane(wn)
        first, last = lanes < z, lanes >= LANES - z
        rows = lax.broadcasted_iota(jnp.int32, (wn, LANES), 0) + (w0 - HY) + gy0
        inside_y = (rows >= 0) & (rows < ycount)
        w = slice(w0, w0 + wn)
        wm = slice(w0 - 1, w0 + wn - 1)
        wp = slice(w0 + 1, w0 + wn + 1)

        def body(i, carry):
            centre = self.k[i, w, :]
            behind = self.k[i, wm, :]
            ahead = self.k[i, wp, :]
            up, down = self.k[i + 1, w, :], self.k[i - 1, w, :]
            zp = jnp.where(last, 0.0, roll(centre, -z))
            zm = jnp.where(first, 0.0, roll(centre, z))
            total = 3.0 * centre + 0.5 * ((up + down) + (ahead + behind) + (zp + zm))
            diag = s * total + self.rea[i, w, :]
            self.dg[i, w, :] = diag
            self.kx[i, w, :] = (0.5 * s) * (centre + up)
            self.ky[i, wm, :] = (0.5 * s) * (behind + centre)
            self.kz[i, w, :] = jnp.where(last, 0.0, (0.5 * s) * (centre + zp))
            self.kzm[i, w, :] = jnp.where(first, 0.0, (0.5 * s) * (centre + zm))
            row = gx0 + i - HX
            inside = inside_y & (row >= 0) & (row < xcount)
            self.inv[i, w, :] = jnp.where(inside, 1.0 / (diag + 2.0 * BETA * s), 0.0)
            return carry

        lax.fori_loop(HX - halo, HX + self.xsize + halo, body, 0)

    def sweep(self, src, halo, window, consume):
        w0, wn = window
        z = self.group
        bs = BETA * self.scale
        lanes = lane(wn)
        first, last = lanes < z, lanes >= LANES - z
        w = slice(w0, w0 + wn)
        wm = slice(w0 - 1, w0 + wn - 1)
        wp = slice(w0 + 1, w0 + wn + 1)

        def div(i, rows, rows_next):
            uz = src[2, i, rows, :]
            total = src[0, i + 1, rows, :] - src[0, i, rows, :]
            total = total + (src[1, i, rows_next, :] - src[1, i, rows, :])
            return bs * (total + (jnp.where(last, 0.0, roll(uz, -z)) - uz))

        def body(i, before):
            here = div(i, w, wp)
            beside = div(i, wm, w)
            u = [src[c, i, w, :] for c in range(3)]
            under = jnp.where(first, bs * u[2], roll(here, z))
            gradients = (before, beside, under)
            kxp, kxm = self.kx[i, w, :], self.kx[i - 1, w, :]
            kyp, kym = self.ky[i, w, :], self.ky[i, wm, :]
            kzp, kzm = self.kz[i, w, :], self.kzm[i, w, :]
            dg = self.dg[i, w, :]
            out = []
            for c in range(3):
                near = kxp * src[c, i + 1, w, :] + kxm * src[c, i - 1, w, :]
                near = near + (kyp * src[c, i, wp, :] + kym * src[c, i, wm, :])
                near = near + (kzp * roll(u[c], -z) + kzm * roll(u[c], z))
                out.append(dg * u[c] - near + (gradients[c] - here))
            consume(i, w, u, out)
            return here

        lo = HX - halo
        lax.fori_loop(lo, HX + self.xsize + halo, body, div(lo - 1, w, wp))

    def step(self, src, dst, halo, number, window=None, out=None):
        rates = rate_list()

        def consume(i, w, u, au):
            inv = self.inv[i, w, :]
            for c in range(3):
                resid = self.f[c, i, w, :] - au[c]
                if number == 0:
                    p = (1.0 / THETA) * (inv * resid)
                else:
                    p = rates[number] * rates[number - 1] * self.p[c, i, w, :]
                    p = p + (2.0 * rates[number] / DELTA) * (inv * resid)
                if number < 3:
                    self.p[c, i, w, :] = p
                if out is not None:
                    out[c, i - HX] = u[c] + p
                else:
                    dst[c, i, w, :] = u[c] + p

        self.sweep(src, halo, window or self.window, consume)

    def first_direction(self, halo):
        w0, wn = self.window
        w = slice(w0, w0 + wn)

        def body(i, carry):
            inv = self.inv[i, w, :]
            for c in range(3):
                p = (1.0 / THETA) * (inv * self.f[c, i, w, :])
                self.p[c, i, w, :] = p
                self.xa[c, i, w, :] = p
            return carry

        lax.fori_loop(HX - halo, HX + self.xsize + halo, body, 0)

    def smooth_down(self, halo):
        self.step(self.xa, self.xb, max(halo - 1, 0), 1)
        self.step(self.xb, self.xa, max(halo - 2, 0), 2)
        self.step(self.xa, self.xb, max(halo - 3, 0), 3)

    def residual(self):
        def consume(i, w, u, au):
            for c in range(3):
                self.p[c, i, w, :] = self.f[c, i, w, :] - au[c]

        self.sweep(self.xb, 0, (HY, round8(self.ysize)), consume)

    def add_grown(self, coarse, xoff, yoff, temp):
        w0, wn = self.window
        w = slice(w0, w0 + wn)
        y0 = HY + (w0 - HY) // 2

        def body(j, carry):
            rows = pl.ds(yoff + y0, wn // 2)
            for c in range(3):
                value = coarse[c, j + (xoff + HX - 2), rows, :]
                temp[pl.ds(0, wn // 2, stride=2), :] = value
                temp[pl.ds(1, wn // 2, stride=2), :] = value
                grown = temp[0:wn, :]
                for t in range(2):
                    i = HX - 4 + 2 * j + t
                    self.xa[c, i, w, :] = self.xb[c, i, w, :] + grown
            return carry

        lax.fori_loop(0, (self.xsize + 8) // 2, body, 0)


def shrink_rows(load, xsize, ysize, group, store):
    def body(j, carry):
        total = None
        for x in range(2):
            for y in range(2):
                value = load(2 * j + x, y, ysize // 2)
                total = value if total is None else total + value
        store(j, 0.125 * halve_lanes(total, group))
        return carry

    lax.fori_loop(0, xsize // 2, body, 0)


def plan(xsize, ysize, groups, bricks):
    levels = []
    for number in range(3):
        size = ysize >> number
        levels.append(Level(number, xsize >> number, size, (HY - 4, round8(size + 8))))
    coarse = (xsize >> 3) * groups, (ysize >> 3) * bricks
    levels.append(Level(3, coarse[0], coarse[1], (HY, round8(coarse[1]))))
    size = xsize
    exchanges = dict(
        e0=Exchange(size, 1, 5, (4, 4, 4, 4, 5)),
        c1=Exchange(size // 2, 2, 3, (4, 5)),
        c2=Exchange(size // 4, 4, 1, (4, 4)),
        f1=Exchange(size // 2, 2, 2, (4, 4, 4)),
        f2=Exchange(size // 4, 4, 1, (4,) * 6),
        x0=Exchange(size, 1, 4, (4, 4, 4)),
        x1=Exchange(size // 2, 2, 2, (4, 4, 4)),
        x2=Exchange(size // 4, 4, 1, (4, 4, 4)),
        y2=Exchange(size // 4, 4, 1, (2, 2, 2)),
        y1=Exchange(size // 2, 2, 1, (2, 2, 2)),
    )
    return levels, exchanges


def cycle(groups, bricks, xsize, ysize, f_in, k_in, rea_in, out, *scratch):
    levels, exchanges = plan(xsize, ysize, groups, bricks)
    devices = groups * bricks
    g, b = lax.axis_index("grp"), lax.axis_index("brick")
    me = g * bricks + b
    exists = {}
    for dx, dy in DIRS:
        good = None
        for d, at, count in ((dx, g, groups), (dy, b, bricks)):
            if d:
                test = at > 0 if d < 0 else at < count - 1
                good = test if good is None else good & test
        exists[(dx, dy)] = good
    scratch = list(scratch)

    def take(count):
        got = scratch[:count]
        del scratch[:count]
        return got

    for level in levels:
        level.bind(take(12))
    for name in exchanges:
        exchanges[name].bind(take(6), (g, b, exists))
    temp, small, slot, slots, slot_send, slot_recv = take(6)
    ex = exchanges
    l0, l1, l2, l3 = levels

    barrier = pltpu.get_barrier_semaphore()

    def partner(n):
        other = (me + n) % devices
        return other // bricks, other % bricks

    def greet(n, carry):
        pl.semaphore_signal(
            barrier, inc=1, device_id=partner(n), device_id_type=pl.DeviceIdType.MESH
        )
        return carry

    lax.fori_loop(1, devices, greet, 0)

    def get_input(field, i, r0, count):
        rows = slice(r0, r0 + count)
        if field < 3:
            return f_in[field, i, rows, :]
        return (rea_in if field == 3 else k_in)[i, rows, :]

    ex["e0"].stage(get_input)
    pl.semaphore_wait(barrier, devices - 1)
    ex["e0"].start()

    for level in levels:
        level.clear()

    def load_own(i, carry):
        own = slice(HY, HY + ysize)
        for c in range(3):
            l0.f[c, HX + i, own, :] = f_in[c, i]
        l0.k[HX + i, own, :] = k_in[i]
        l0.rea[HX + i, own, :] = rea_in[i]
        return carry

    lax.fori_loop(0, xsize, load_own, 0)

    def shrink_field(fine, coarse, ref, target):
        def load(x, y, count):
            return ref[HX + x, pl.ds(HY + y, count, stride=2), :]

        def store(j, value):
            target[HX + j, HY : HY + value.shape[0], :] = value

        shrink_rows(load, fine.xsize, fine.ysize, fine.group, store)

    for fine, coarse in ((l0, l1), (l1, l2)):
        shrink_field(fine, coarse, fine.k, coarse.k)
        shrink_field(fine, coarse, fine.rea, coarse.rea)

    def getter(*refs):
        def get(field, i, r0, count):
            ref, c = refs[field]
            rows = slice(HY + r0, HY + r0 + count)
            return ref[HX + i, rows, :] if c is None else ref[c, HX + i, rows, :]

        return get

    def putter(*refs):
        def put(field, i, r0, value):
            ref, c = refs[field]
            rows = slice(HY + r0, HY + r0 + value.shape[0])
            if c is None:
                ref[HX + i, rows, :] = value
            else:
                ref[c, HX + i, rows, :] = value

        return put

    def three(ref):
        return tuple((ref, c) for c in range(3))

    def own_prepare(level, halo):
        xs, ys = level.xsize, level.ysize
        level.prepare(halo, g * xs, b * ys, xs * groups, ys * bricks)

    ex["c1"].stage(getter((l1.rea, None), (l1.k, None)))
    ex["c2"].stage(getter((l2.rea, None), (l2.k, None)))
    ex["e0"].finish(putter(*three(l0.f), (l0.rea, None), (l0.k, None)))
    ex["c1"].start()
    ex["c2"].start()

    def shrink_residual(fine, coarse):
        for c in range(3):
            shrink_field(fine, coarse, fine.p.at[c], coarse.f.at[c])

    own_prepare(l0, 4)
    l0.first_direction(4)
    l0.smooth_down(4)
    l0.residual()
    shrink_residual(l0, l1)

    ex["f1"].stage(getter(*three(l1.f)))
    ex["f1"].start()
    ex["x0"].stage(getter(*three(l0.xb)))
    ex["c1"].finish(putter((l1.rea, None), (l1.k, None)))
    ex["c2"].finish(putter((l2.rea, None), (l2.k, None)))
    own_prepare(l1, 4)
    own_prepare(l2, 4)
    ex["f1"].finish(putter(*three(l1.f)))
    ex["x0"].start()
    l1.first_direction(4)
    l1.smooth_down(4)
    l1.residual()
    shrink_residual(l1, l2)

    l2.first_direction(0)
    ex["f2"].stage(getter(*three(l2.f), *three(l2.p)))
    ex["f2"].start()
    ex["x1"].stage(getter(*three(l1.xb)))

    def put_f2(field, i, r0, value):
        putter(*three(l2.f), *three(l2.p))(field, i, r0, value)
        if field >= 3:
            putter(*three(l2.xa))(field - 3, i, r0, value)

    ex["f2"].finish(put_f2)
    ex["x1"].start()
    l2.smooth_down(4)
    ex["x2"].stage(getter(*three(l2.xb)))
    ex["x2"].start()
    l2.residual()

    def load_fine(field, x, y):
        rows = slice(HY + y, HY + y + 1)
        if field < 3:
            return l2.p[field, HX + x, rows, :]
        return (l2.rea if field == 3 else l2.k)[HX + x, rows, :]

    slot[...] = jnp.zeros_like(slot)
    for field in range(5):
        values = []
        for x in range(2):
            for y in range(2):
                total = load_fine(field, 2 * x, 2 * y) + load_fine(field, 2 * x, 2 * y + 1)
                total = total + load_fine(field, 2 * x + 1, 2 * y)
                total = total + load_fine(field, 2 * x + 1, 2 * y + 1)
                values.append(0.125 * halve_lanes(total, 4))
        slot[field : field + 1, :] = pack(values, 8)

    def gather_copy(n):
        return pltpu.make_async_remote_copy(
            src_ref=slot,
            dst_ref=slots.at[me],
            send_sem=slot_send.at[n],
            recv_sem=slot_recv.at[me],
            device_id=partner(n),
            device_id_type=pl.DeviceIdType.MESH,
        )

    def send_slot(n, carry):
        gather_copy(n).start()
        return carry

    lax.fori_loop(1, devices, send_slot, 0)

    def place(value, owner):
        og, ob = owner // bricks, owner % bricks
        for x in range(2):
            for y in range(2):
                small[...] = unpack(value, 8, 2 * x + y)
                row, col = HX + 2 * og + x, HY + 2 * ob + y
                for field in range(5):
                    line = small[field : field + 1, :]
                    if field < 3:
                        l3.f[field, row, pl.ds(col, 1), :] = line
                    else:
                        (l3.rea if field == 3 else l3.k)[row, pl.ds(col, 1), :] = line

    place(slot[...], me)

    def receive(n, carry):
        owner = (me + n) % devices
        pltpu.make_async_remote_copy(
            src_ref=slot,
            dst_ref=slots.at[owner],
            send_sem=slot_send.at[n],
            recv_sem=slot_recv.at[owner],
            device_id=partner(n),
            device_id_type=pl.DeviceIdType.MESH,
        ).wait_recv()
        place(slots[owner], owner)
        return carry

    lax.fori_loop(1, devices, receive, 0)
    l3.prepare(0, 0, 0, l3.xsize, l3.ysize)
    edge = slice(l3.window[0], l3.window[0] + l3.window[1])
    l3.kx[HX - 1, edge, :] = (0.5 * l3.scale) * l3.k[HX, edge, :]
    l3.first_direction(0)
    l3.smooth_down(0)

    ex["x2"].finish(putter(*three(l2.xb)))
    l2.add_grown(l3.xb, g * (xsize // 8), b * (ysize // 8), temp)
    up(l2)
    ex["y2"].stage(getter(*three(l2.xa)))
    ex["y2"].start()
    ex["x1"].finish(putter(*three(l1.xb)))
    ex["y2"].finish(putter(*three(l2.xa)))
    l1.add_grown(l2.xa, 0, 0, temp)
    up(l1)
    ex["y1"].stage(getter(*three(l1.xa)))
    ex["y1"].start()
    ex["x0"].finish(putter(*three(l0.xb)))
    ex["y1"].finish(putter(*three(l1.xa)))
    l0.add_grown(l1.xa, 0, 0, temp)
    up(l0, out)

    for name in ex:
        ex[name].finish_send()

    def sent(n, carry):
        gather_copy(n).wait_send()
        return carry

    lax.fori_loop(1, devices, sent, 0)


def up(level, out=None):
    level.step(level.xa, level.xb, 3, 0)
    level.step(level.xb, level.xa, 2, 1)
    level.step(level.xa, level.xb, 1, 2)
    level.step(level.xb, level.xa, 0, 3, (HY, round8(level.ysize)), out)


def on_device(right_side, stiffness, reaction):
    groups, bricks = lax.axis_size("grp"), lax.axis_size("brick")
    _, xsize, ysize, _ = right_side.shape
    levels, exchanges = plan(xsize, ysize, groups, bricks)
    devices = groups * bricks
    scratch = []
    for level in levels:
        scratch += level.scratch()
    for name in exchanges:
        scratch += exchanges[name].scratch()
    scratch += [
        pltpu.VMEM((32, LANES), jnp.float32),
        pltpu.VMEM((8, LANES), jnp.float32),
        pltpu.VMEM((8, LANES), jnp.float32),
        pltpu.VMEM((devices, 8, LANES), jnp.float32),
        pltpu.SemaphoreType.DMA((devices,)),
        pltpu.SemaphoreType.DMA((devices,)),
    ]

    def kernel(*refs):
        cycle(groups, bricks, xsize, ysize, *refs)

    vmem = pl.BlockSpec(memory_space=pltpu.VMEM)
    return pl.pallas_call(
        kernel,
        out_shape=jax.ShapeDtypeStruct(right_side.shape, jnp.float32),
        in_specs=[vmem] * 3,
        out_specs=vmem,
        scratch_shapes=scratch,
        compiler_params=pltpu.CompilerParams(
            collective_id=0, has_side_effects=True, vmem_limit_bytes=56 * 2**20
        ),
    )(right_side, stiffness, reaction)


def solution(mesh):
    in_specs = (P(None, "grp", "brick", None), P("grp", "brick", None), P("grp", "brick", None))
    out_specs = P(None, "grp", "brick", None)
    return jax.shard_map(
        on_device, mesh=mesh, in_specs=in_specs, out_specs=out_specs, check_vma=False
    )
```

time: 599 us -> 118 us (0.20)
  the two profiles are of different devices: /device:TPU:28 before, /device:TPU:1 now
where the time goes in v1:
time: 118 us
  Pallas kernels  116 us (98%)
  local copies, waits for them, and re-layouts  1.77 us (2%)
    pallas_call x1, Pallas kernels, on_device(): pl.pallas_call(kernel, out_shape=jax.ShapeDtypeStruct(right_side.shape, j...  116 us

profile of v1, /device:TPU:1, one launch (start us, length us, event | category | flops | bytes accessed | tf_op | source)
XLA Modules:
  0.0 118.0 jit_solution(13081227618113775416)
XLA Ops:
  0.0 116.2 %shard_map.37 = f32[3,16,16,128]{3,2,1,0:T(8,128)} custom-call(f32[3,16,16,128]{3,2,1,0:T(8,128)} %refs_0_.1, f32[16,16,128]{2,1,0:T(8,128)} %refs_1_.1, f32[16,16,128]{2,1,0:T(8,128)} %refs_2_.1), custom_call_target="tpu_custom_call" | custom-call | tf_op jit(solution)/shard_map/pallas_call | solution.py:683
  116.2 1.8 %copy.5 = f32[3,16,16,128]{3,2,1,0:T(8,128)} copy(f32[3,16,16,128]{3,2,1,0:T(8,128)} %shard_map.37) | data formatting | bytes 786432

commit v2 on v1

--- a/solution.py
+++ b/solution.py
@@ -62,44 +62,51 @@
     return value + jnp.where(first, roll(value, -group), roll(value, group))
 
 
+def rows_loop(start, count, most, body, carry=None):
+    each = max(n for n in range(1, most + 1) if count % n == 0)
+    if count == each:
+        return body([start + t for t in range(each)], carry)
+
+    def step(n, carry):
+        out = body([start + n * each + t for t in range(each)], carry)
+        return 0 if out is None else out
+
+    return lax.fori_loop(0, count // each, step, 0 if carry is None else carry)
+
+
 class Exchange:
     def __init__(self, size, group, packed, widths):
         self.size, self.group, self.packed, self.widths = size, group, packed, widths
         self.blocks = size // group
         self.offs = [sum(widths[:n]) for n in range(len(widths))]
-        self.rows = round8(sum(widths))
-        self.xrows = round8(len(widths) * size)
+        self.width = sum(widths)
+        self.side_rows = round8(self.blocks * self.width)
+        self.corner_rows = round8(packed * self.width)
+        self.front_rows = round8(packed * len(widths) * size)
 
     def scratch(self):
-        f32 = jnp.float32
-        return [
-            pltpu.VMEM((2, self.packed, self.xrows, LANES), f32),
-            pltpu.VMEM((2, self.blocks, self.rows, LANES), f32),
-            pltpu.VMEM((2, self.packed, self.xrows, LANES), f32),
-            pltpu.VMEM((2, self.blocks + 2 * self.packed, self.rows, LANES), f32),
-            pltpu.SemaphoreType.DMA((8,)),
-            pltpu.SemaphoreType.DMA((8,)),
+        both = [
+            pltpu.VMEM((2, self.front_rows, LANES), jnp.float32),
+            pltpu.VMEM((2, self.side_rows, LANES), jnp.float32),
+            pltpu.VMEM((4, self.corner_rows, LANES), jnp.float32),
         ]
+        return both + both + [pltpu.SemaphoreType.DMA((8,)), pltpu.SemaphoreType.DMA((8,))]
 
     def bind(self, refs, where):
-        self.sx, self.sy, self.rx, self.ry, self.ssem, self.rsem = refs
+        self.sx, self.sy, self.sc, self.rx, self.ry, self.rc, self.ssem, self.rsem = refs
         self.where = where
 
     def copy(self, ex, ey):
         g, b, _ = self.where
-        n, w = self.blocks, self.packed
         if ey == 0:
             side = 0 if ex < 0 else 1
             src, dst = self.sx.at[side], self.rx.at[1 - side]
-        else:
+        elif ex == 0:
             side = 0 if ey < 0 else 1
             src, dst = self.sy.at[side], self.ry.at[1 - side]
-            if ex == 0:
-                dst = dst.at[pl.ds(w, n)]
-            elif ex < 0:
-                src, dst = src.at[pl.ds(0, w)], dst.at[pl.ds(w + n, w)]
-            else:
-                src, dst = src.at[pl.ds(n - w, w)], dst.at[pl.ds(0, w)]
+        else:
+            side = (1 if ex > 0 else 0) * 2 + (1 if ey > 0 else 0)
+            src, dst = self.sc.at[side], self.rc.at[3 - side]
         return pltpu.make_async_remote_copy(
             src_ref=src,
             dst_ref=dst,
@@ -110,27 +117,28 @@
         )
 
     def stage(self, get):
-        def put(j, field, r0, count, ref, side, row, off):
-            values = [get(field, j * self.group + t, r0, count) for t in range(self.group)]
-            ref[side, row, off : off + count, :] = pack(values, self.group)
-
-        def body(j, carry):
+        size, group, last = self.size, self.group, self.blocks - self.packed
+
+        def load(field, j, r0, count):
+            return pack([get(field, j * group + t, r0, count) for t in range(group)], group)
+
+        for j in range(self.blocks):
             for field, width in enumerate(self.widths):
                 for side in (0, 1):
-                    r0 = 0 if side == 0 else self.size - width
-                    put(j, field, r0, width, self.sy, side, j, self.offs[field])
-            return carry
-
-        if self.blocks > 4:
-            lax.fori_loop(0, self.blocks, body, 0)
-        else:
-            for j in range(self.blocks):
-                body(j, 0)
+                    value = load(field, j, 0 if side == 0 else size - width, width)
+                    at = j * self.width + self.offs[field]
+                    self.sy[side, at : at + width, :] = value
+                    if j < self.packed:
+                        self.sc[side, at : at + width, :] = value
+                    if j >= last:
+                        at = (j - last) * self.width + self.offs[field]
+                        self.sc[2 + side, at : at + width, :] = value
         for side in (0, 1):
             for j in range(self.packed):
                 for field in range(len(self.widths)):
-                    at = j if side == 0 else self.blocks - self.packed + j
-                    put(at, field, 0, self.size, self.sx, side, j, field * self.size)
+                    at = (j * len(self.widths) + field) * size
+                    value = load(field, j if side == 0 else last + j, 0, size)
+                    self.sx[side, at : at + size, :] = value
 
     def start(self):
         exists = self.where[2]
@@ -150,8 +158,7 @@
         exists = self.where[2]
         size, group = self.size, self.group
 
-        def spread_rows(ref, side, row, x0, off, field, y0, count):
-            value = ref[side, row, off : off + count, :]
+        def spread_rows(value, x0, field, y0):
             for t in range(group):
                 put(field, x0 + t, y0, unpack(value, group, t))
 
@@ -160,42 +167,22 @@
             def _(d=d):
                 dx, dy = d
                 self.copy(-dx, -dy).wait_recv()
-                if dy == 0:
-                    side = 0 if dx < 0 else 1
-                    base = -self.packed * group if dx < 0 else size
-                    for j in range(self.packed):
-                        for field in range(len(self.widths)):
-                            spread_rows(
-                                self.rx, side, j, base + j * group, field * size, field, 0, size
-                            )
-                    return
-                side = 0 if dy < 0 else 1
-                first, count = {
-                    -1: (0, self.packed),
-                    0: (self.packed, self.blocks),
-                    1: (self.packed + self.blocks, self.packed),
-                }[dx]
-
-                def body(j, carry):
+                xside, yside = (0 if dx < 0 else 1), (0 if dy < 0 else 1)
+                base = {-1: -self.packed * group, 0: 0, 1: size}[dx]
+                for j in range(self.packed if dx else self.blocks):
                     for field, width in enumerate(self.widths):
-                        y0 = -width if dy < 0 else size
-                        spread_rows(
-                            self.ry,
-                            side,
-                            first + j,
-                            (first + j - self.packed) * group,
-                            self.offs[field],
-                            field,
-                            y0,
-                            width,
-                        )
-                    return carry
-
-                if count > 4:
-                    lax.fori_loop(0, count, body, 0)
-                else:
-                    for j in range(count):
-                        body(j, 0)
+                        if dy == 0:
+                            at = (j * len(self.widths) + field) * size
+                            value, y0 = self.rx[xside, at : at + size, :], 0
+                        else:
+                            at = j * self.width + self.offs[field]
+                            rows = slice(at, at + width)
+                            if dx == 0:
+                                value = self.ry[yside, rows, :]
+                            else:
+                                value = self.rc[2 * xside + yside, rows, :]
+                            y0 = -width if dy < 0 else size
+                        spread_rows(value, base + j * group, field, y0)
 
 
 class Level:
@@ -243,7 +230,7 @@
         wm = slice(w0 - 1, w0 + wn - 1)
         wp = slice(w0 + 1, w0 + wn + 1)
 
-        def body(i, carry):
+        def one(i):
             centre = self.k[i, w, :]
             behind = self.k[i, wm, :]
             ahead = self.k[i, wp, :]
@@ -252,17 +239,27 @@
             zm = jnp.where(first, 0.0, roll(centre, z))
             total = 3.0 * centre + 0.5 * ((up + down) + (ahead + behind) + (zp + zm))
             diag = s * total + self.rea[i, w, :]
-            self.dg[i, w, :] = diag
-            self.kx[i, w, :] = (0.5 * s) * (centre + up)
-            self.ky[i, wm, :] = (0.5 * s) * (behind + centre)
-            self.kz[i, w, :] = jnp.where(last, 0.0, (0.5 * s) * (centre + zp))
-            self.kzm[i, w, :] = jnp.where(first, 0.0, (0.5 * s) * (centre + zm))
             row = gx0 + i - HX
             inside = inside_y & (row >= 0) & (row < xcount)
-            self.inv[i, w, :] = jnp.where(inside, 1.0 / (diag + 2.0 * BETA * s), 0.0)
-            return carry
-
-        lax.fori_loop(HX - halo, HX + self.xsize + halo, body, 0)
+            return (
+                diag,
+                (0.5 * s) * (centre + up),
+                (0.5 * s) * (behind + centre),
+                jnp.where(last, 0.0, (0.5 * s) * (centre + zp)),
+                jnp.where(first, 0.0, (0.5 * s) * (centre + zm)),
+                jnp.where(inside, 1.0 / (diag + 2.0 * BETA * s), 0.0),
+            )
+
+        def body(rows, carry):
+            for i, values in [(i, one(i)) for i in rows]:
+                self.dg[i, w, :] = values[0]
+                self.kx[i, w, :] = values[1]
+                self.ky[i, wm, :] = values[2]
+                self.kz[i, w, :] = values[3]
+                self.kzm[i, w, :] = values[4]
+                self.inv[i, w, :] = values[5]
+
+        rows_loop(HX - halo, self.xsize + 2 * halo, 4, body)
 
     def sweep(self, src, halo, window, consume):
         w0, wn = window
@@ -274,17 +271,22 @@
         wm = slice(w0 - 1, w0 + wn - 1)
         wp = slice(w0 + 1, w0 + wn + 1)
 
-        def div(i, rows, rows_next):
-            uz = src[2, i, rows, :]
+        def flat(i, rows, rows_next):
             total = src[0, i + 1, rows, :] - src[0, i, rows, :]
-            total = total + (src[1, i, rows_next, :] - src[1, i, rows, :])
-            return bs * (total + (jnp.where(last, 0.0, roll(uz, -z)) - uz))
-
-        def body(i, before):
-            here = div(i, w, wp)
-            beside = div(i, wm, w)
+            return total + (src[1, i, rows_next, :] - src[1, i, rows, :])
+
+        def div(part, uz, ahead):
+            return bs * (part + (jnp.where(last, 0.0, ahead) - uz))
+
+        def one(i, before):
             u = [src[c, i, w, :] for c in range(3)]
-            under = jnp.where(first, bs * u[2], roll(here, z))
+            ahead = [roll(u[c], -z) for c in range(3)]
+            behind = [roll(u[c], z) for c in range(3)]
+            part = flat(i, w, wp)
+            here = div(part, u[2], ahead[2])
+            side_z = src[2, i, wm, :]
+            beside = div(flat(i, wm, w), side_z, roll(side_z, -z))
+            under = bs * (u[2] + jnp.where(first, 0.0, roll(part - u[2], z)))
             gradients = (before, beside, under)
             kxp, kxm = self.kx[i, w, :], self.kx[i - 1, w, :]
             kyp, kym = self.ky[i, w, :], self.ky[i, wm, :]
@@ -294,19 +296,31 @@
             for c in range(3):
                 near = kxp * src[c, i + 1, w, :] + kxm * src[c, i - 1, w, :]
                 near = near + (kyp * src[c, i, wp, :] + kym * src[c, i, wm, :])
-                near = near + (kzp * roll(u[c], -z) + kzm * roll(u[c], z))
+                near = near + (kzp * ahead[c] + kzm * behind[c])
                 out.append(dg * u[c] - near + (gradients[c] - here))
-            consume(i, w, u, out)
-            return here
+            return consume(i, w, u, out), here
+
+        def body(rows, before):
+            stores = []
+            for i in rows:
+                more, before = one(i, before)
+                stores += more
+            for ref, index, value in stores:
+                ref[index] = value
+            return before
 
         lo = HX - halo
-        lax.fori_loop(lo, HX + self.xsize + halo, body, div(lo - 1, w, wp))
+        uz = src[2, lo - 1, w, :]
+        before = div(flat(lo - 1, w, wp), uz, roll(uz, -z))
+        most = 4 if self.number == 0 else 7
+        rows_loop(lo, self.xsize + 2 * halo, most, body, before)
 
     def step(self, src, dst, halo, number, window=None, out=None):
         rates = rate_list()
 
         def consume(i, w, u, au):
             inv = self.inv[i, w, :]
+            stores = []
             for c in range(3):
                 resid = self.f[c, i, w, :] - au[c]
                 if number == 0:
@@ -314,12 +328,14 @@
                 else:
                     p = rates[number] * rates[number - 1] * self.p[c, i, w, :]
                     p = p + (2.0 * rates[number] / DELTA) * (inv * resid)
+                at = (c, i, w, slice(None))
                 if number < 3:
-                    self.p[c, i, w, :] = p
+                    stores.append((self.p, at, p))
                 if out is not None:
-                    out[c, i - HX] = u[c] + p
+                    stores.append((out, (c, i - HX), u[c] + p))
                 else:
-                    dst[c, i, w, :] = u[c] + p
+                    stores.append((dst, at, u[c] + p))
+            return stores
 
         self.sweep(src, halo, window or self.window, consume)
 
@@ -327,15 +343,16 @@
         w0, wn = self.window
         w = slice(w0, w0 + wn)
 
-        def body(i, carry):
-            inv = self.inv[i, w, :]
-            for c in range(3):
-                p = (1.0 / THETA) * (inv * self.f[c, i, w, :])
+        def body(rows, carry):
+            stores = []
+            for i in rows:
+                inv = (1.0 / THETA) * self.inv[i, w, :]
+                stores += [(i, c, inv * self.f[c, i, w, :]) for c in range(3)]
+            for i, c, p in stores:
                 self.p[c, i, w, :] = p
                 self.xa[c, i, w, :] = p
-            return carry
-
-        lax.fori_loop(HX - halo, HX + self.xsize + halo, body, 0)
+
+        rows_loop(HX - halo, self.xsize + 2 * halo, 4, body)
 
     def smooth_down(self, halo):
         self.step(self.xa, self.xb, max(halo - 1, 0), 1)
@@ -344,42 +361,47 @@
 
     def residual(self):
         def consume(i, w, u, au):
-            for c in range(3):
-                self.p[c, i, w, :] = self.f[c, i, w, :] - au[c]
+            at = [(c, i, w, slice(None)) for c in range(3)]
+            return [(self.p, at[c], self.f[c, i, w, :] - au[c]) for c in range(3)]
 
         self.sweep(self.xb, 0, (HY, round8(self.ysize)), consume)
 
     def add_grown(self, coarse, xoff, yoff, temp):
         w0, wn = self.window
         w = slice(w0, w0 + wn)
-        y0 = HY + (w0 - HY) // 2
-
-        def body(j, carry):
-            rows = pl.ds(yoff + y0, wn // 2)
-            for c in range(3):
-                value = coarse[c, j + (xoff + HX - 2), rows, :]
-                temp[pl.ds(0, wn // 2, stride=2), :] = value
-                temp[pl.ds(1, wn // 2, stride=2), :] = value
-                grown = temp[0:wn, :]
-                for t in range(2):
-                    i = HX - 4 + 2 * j + t
-                    self.xa[c, i, w, :] = self.xb[c, i, w, :] + grown
-            return carry
-
-        lax.fori_loop(0, (self.xsize + 8) // 2, body, 0)
-
-
-def shrink_rows(load, xsize, ysize, group, store):
-    def body(j, carry):
-        total = None
-        for x in range(2):
-            for y in range(2):
-                value = load(2 * j + x, y, ysize // 2)
-                total = value if total is None else total + value
-        store(j, 0.125 * halve_lanes(total, group))
-        return carry
-
-    lax.fori_loop(0, xsize // 2, body, 0)
+        half = wn // 2
+        rows = pl.ds(yoff + HY + (w0 - HY) // 2, half)
+
+        def body(js, carry):
+            for n, j in enumerate(js):
+                for c in range(3):
+                    value = coarse[c, j + (xoff + HX - 2), rows, :]
+                    temp[3 * n + c, pl.ds(0, half, stride=2), :] = value
+                    temp[3 * n + c, pl.ds(1, half, stride=2), :] = value
+            for n, j in enumerate(js):
+                for c in range(3):
+                    grown = temp[3 * n + c, 0:wn, :]
+                    for t in range(2):
+                        i = HX - 4 + 2 * j + t
+                        self.xa[c, i, w, :] = self.xb[c, i, w, :] + grown
+
+        rows_loop(0, (self.xsize + 8) // 2, 4, body)
+
+
+def shrink_fields(fine, pairs):
+    half = fine.ysize // 2
+
+    def body(js, carry):
+        values = []
+        for j in js:
+            for load, store in pairs:
+                total = load(2 * j, 0, half) + load(2 * j, 1, half)
+                total = total + (load(2 * j + 1, 0, half) + load(2 * j + 1, 1, half))
+                values.append((store, j, 0.125 * halve_lanes(total, fine.group)))
+        for store, j, value in values:
+            store(j, value)
+
+    rows_loop(0, fine.xsize // 2, 4, body)
 
 
 def plan(xsize, ysize, groups, bricks):
@@ -391,7 +413,8 @@
     levels.append(Level(3, coarse[0], coarse[1], (HY, round8(coarse[1]))))
     size = xsize
     exchanges = dict(
-        e0=Exchange(size, 1, 5, (4, 4, 4, 4, 5)),
+        c0=Exchange(size, 1, 5, (4, 5)),
+        f0=Exchange(size, 1, 4, (4, 4, 4)),
         c1=Exchange(size // 2, 2, 3, (4, 5)),
         c2=Exchange(size // 4, 4, 1, (4, 4)),
         f1=Exchange(size // 2, 2, 2, (4, 4, 4)),
@@ -428,8 +451,8 @@
     for level in levels:
         level.bind(take(12))
     for name in exchanges:
-        exchanges[name].bind(take(6), (g, b, exists))
-    temp, small, slot, slots, slot_send, slot_recv = take(6)
+        exchanges[name].bind(take(8), (g, b, exists))
+    temp, slot, slots, slot_send, slot_recv = take(5)
     ex = exchanges
     l0, l1, l2, l3 = levels
 
@@ -447,15 +470,17 @@
 
     lax.fori_loop(1, devices, greet, 0)
 
-    def get_input(field, i, r0, count):
-        rows = slice(r0, r0 + count)
-        if field < 3:
-            return f_in[field, i, rows, :]
-        return (rea_in if field == 3 else k_in)[i, rows, :]
-
-    ex["e0"].stage(get_input)
+    def get_coeff(field, i, r0, count):
+        return (rea_in, k_in)[field][i, r0 : r0 + count, :]
+
+    def get_source(field, i, r0, count):
+        return f_in[field, i, r0 : r0 + count, :]
+
+    ex["c0"].stage(get_coeff)
     pl.semaphore_wait(barrier, devices - 1)
-    ex["e0"].start()
+    ex["c0"].start()
+    ex["f0"].stage(get_source)
+    ex["f0"].start()
 
     for level in levels:
         level.clear()
@@ -470,18 +495,18 @@
 
     lax.fori_loop(0, xsize, load_own, 0)
 
-    def shrink_field(fine, coarse, ref, target):
+    def shrink_pair(ref, target):
         def load(x, y, count):
             return ref[HX + x, pl.ds(HY + y, count, stride=2), :]
 
         def store(j, value):
             target[HX + j, HY : HY + value.shape[0], :] = value
 
-        shrink_rows(load, fine.xsize, fine.ysize, fine.group, store)
+        return load, store
 
     for fine, coarse in ((l0, l1), (l1, l2)):
-        shrink_field(fine, coarse, fine.k, coarse.k)
-        shrink_field(fine, coarse, fine.rea, coarse.rea)
+        pairs = [shrink_pair(fine.k, coarse.k), shrink_pair(fine.rea, coarse.rea)]
+        shrink_fields(fine, pairs)
 
     def getter(*refs):
         def get(field, i, r0, count):
@@ -511,15 +536,16 @@
 
     ex["c1"].stage(getter((l1.rea, None), (l1.k, None)))
     ex["c2"].stage(getter((l2.rea, None), (l2.k, None)))
-    ex["e0"].finish(putter(*three(l0.f), (l0.rea, None), (l0.k, None)))
+    ex["c0"].finish(putter((l0.rea, None), (l0.k, None)))
+
+    def shrink_residual(fine, coarse):
+        pairs = [shrink_pair(fine.p.at[c], coarse.f.at[c]) for c in range(3)]
+        shrink_fields(fine, pairs)
+
+    own_prepare(l0, 4)
+    ex["f0"].finish(putter(*three(l0.f)))
     ex["c1"].start()
     ex["c2"].start()
-
-    def shrink_residual(fine, coarse):
-        for c in range(3):
-            shrink_field(fine, coarse, fine.p.at[c], coarse.f.at[c])
-
-    own_prepare(l0, 4)
     l0.first_direction(4)
     l0.smooth_down(4)
     l0.residual()
@@ -576,7 +602,7 @@
     def gather_copy(n):
         return pltpu.make_async_remote_copy(
             src_ref=slot,
-            dst_ref=slots.at[me],
+            dst_ref=slots.at[pl.ds(me * 8, 8)],
             send_sem=slot_send.at[n],
             recv_sem=slot_recv.at[me],
             device_id=partner(n),
@@ -589,35 +615,32 @@
 
     lax.fori_loop(1, devices, send_slot, 0)
 
-    def place(value, owner):
-        og, ob = owner // bricks, owner % bricks
-        for x in range(2):
-            for y in range(2):
-                small[...] = unpack(value, 8, 2 * x + y)
-                row, col = HX + 2 * og + x, HY + 2 * ob + y
-                for field in range(5):
-                    line = small[field : field + 1, :]
-                    if field < 3:
-                        l3.f[field, row, pl.ds(col, 1), :] = line
-                    else:
-                        (l3.rea if field == 3 else l3.k)[row, pl.ds(col, 1), :] = line
-
-    place(slot[...], me)
+    slots[pl.ds(pl.multiple_of(me * 8, 8), 8), :] = slot[...]
 
     def receive(n, carry):
         owner = (me + n) % devices
         pltpu.make_async_remote_copy(
             src_ref=slot,
-            dst_ref=slots.at[owner],
+            dst_ref=slots.at[pl.ds(owner * 8, 8)],
             send_sem=slot_send.at[n],
             recv_sem=slot_recv.at[owner],
             device_id=partner(n),
             device_id_type=pl.DeviceIdType.MESH,
         ).wait_recv()
-        place(slots[owner], owner)
         return carry
 
     lax.fori_loop(1, devices, receive, 0)
+    for og in range(groups):
+        for field in range(5):
+            value = slots[pl.ds(og * bricks * 8 + field, bricks, stride=8), :]
+            for x in range(2):
+                for y in range(2):
+                    line = unpack(value, 8, 2 * x + y)
+                    row, cols = HX + 2 * og + x, pl.ds(HY + y, bricks, stride=2)
+                    if field < 3:
+                        l3.f[field, row, cols, :] = line
+                    else:
+                        (l3.rea if field == 3 else l3.k)[row, cols, :] = line
     l3.prepare(0, 0, 0, l3.xsize, l3.ysize)
     edge = slice(l3.window[0], l3.window[0] + l3.window[1])
     l3.kx[HX - 1, edge, :] = (0.5 * l3.scale) * l3.k[HX, edge, :]
@@ -668,10 +691,9 @@
     for name in exchanges:
         scratch += exchanges[name].scratch()
     scratch += [
-        pltpu.VMEM((32, LANES), jnp.float32),
+        pltpu.VMEM((12, 32, LANES), jnp.float32),
         pltpu.VMEM((8, LANES), jnp.float32),
-        pltpu.VMEM((8, LANES), jnp.float32),
-        pltpu.VMEM((devices, 8, LANES), jnp.float32),
+        pltpu.VMEM((8 * devices, LANES), jnp.float32),
         pltpu.SemaphoreType.DMA((devices,)),
         pltpu.SemaphoreType.DMA((devices,)),
     ]

time: 118 us -> 69.7 us (0.59)
  Pallas kernels: 116 us -> 67.7 us
    pallas_call x1, Pallas kernels: 116 us -> 67.7 us  [on_device(): pl.pallas_call(kernel, out_shape=jax.ShapeDtypeStruct(right_side.shape, j...]
where the time goes in v2:
time: 69.7 us; the launch traced here: 69.5 us
  Pallas kernels  67.7 us (97%)
  local copies, waits for them, and re-layouts  1.77 us (3%)
    pallas_call x1, Pallas kernels, on_device(): pl.pallas_call(kernel, out_shape=jax.ShapeDtypeStruct(right_side.shape, j...  67.7 us
    unnamed x1, local copies, waits for them, and re-layouts  1.77 us

profile of v2, /device:TPU:1, one launch (start us, length us, event | category | flops | bytes accessed | tf_op | source)
XLA Modules:
  0.0 69.5 jit_solution(7714785688138484285)
XLA Ops:
  0.0 67.7 %shard_map.37 = f32[3,16,16,128]{3,2,1,0:T(8,128)} custom-call(f32[3,16,16,128]{3,2,1,0:T(8,128)} %refs_0_.1, f32[16,16,128]{2,1,0:T(8,128)} %refs_1_.1, f32[16,16,128]{2,1,0:T(8,128)} %refs_2_.1), custom_call_target="tpu_custom_call" | custom-call | tf_op jit(solution)/shard_map/pallas_call | solution.py:705
  67.7 1.8 %copy.5 = f32[3,16,16,128]{3,2,1,0:T(8,128)} copy(f32[3,16,16,128]{3,2,1,0:T(8,128)} %shard_map.37) | data formatting | bytes 786432

commit v3 on v2

--- a/solution.py
+++ b/solution.py
@@ -154,35 +154,41 @@
             def _(d=d):
                 self.copy(*d).wait_send()
 
+    def clear_absent(self):
+        exists = self.where[2]
+        for d in DIRS:
+            @pl.when(jnp.logical_not(exists[d]))
+            def _(d=d):
+                ref = self.landing(*d)
+                ref[...] = jnp.zeros(ref.shape, jnp.float32)
+
+    def landing(self, dx, dy):
+        xside, yside = (0 if dx < 0 else 1), (0 if dy < 0 else 1)
+        if dy == 0:
+            return self.rx.at[xside]
+        return self.ry.at[yside] if dx == 0 else self.rc.at[2 * xside + yside]
+
     def finish(self, put):
         exists = self.where[2]
         size, group = self.size, self.group
-
-        def spread_rows(value, x0, field, y0):
-            for t in range(group):
-                put(field, x0 + t, y0, unpack(value, group, t))
-
-        for d in DIRS:
-            @pl.when(exists[d])
-            def _(d=d):
-                dx, dy = d
+        for dx, dy in DIRS:
+            @pl.when(exists[(dx, dy)])
+            def _(dx=dx, dy=dy):
                 self.copy(-dx, -dy).wait_recv()
-                xside, yside = (0 if dx < 0 else 1), (0 if dy < 0 else 1)
-                base = {-1: -self.packed * group, 0: 0, 1: size}[dx]
-                for j in range(self.packed if dx else self.blocks):
-                    for field, width in enumerate(self.widths):
-                        if dy == 0:
-                            at = (j * len(self.widths) + field) * size
-                            value, y0 = self.rx[xside, at : at + size, :], 0
-                        else:
-                            at = j * self.width + self.offs[field]
-                            rows = slice(at, at + width)
-                            if dx == 0:
-                                value = self.ry[yside, rows, :]
-                            else:
-                                value = self.rc[2 * xside + yside, rows, :]
-                            y0 = -width if dy < 0 else size
-                        spread_rows(value, base + j * group, field, y0)
+
+        for dx, dy in DIRS:
+            ref = self.landing(dx, dy)
+            base = {-1: -self.packed * group, 0: 0, 1: size}[dx]
+            for j in range(self.packed if dx else self.blocks):
+                for field, width in enumerate(self.widths):
+                    if dy == 0:
+                        at, count, y0 = (j * len(self.widths) + field) * size, size, 0
+                    else:
+                        at, count = j * self.width + self.offs[field], width
+                        y0 = -width if dy < 0 else size
+                    value = ref[at : at + count, :]
+                    for t in range(group):
+                        put(field, base + j * group + t, y0, unpack(value, group, t))
 
 
 class Level:
@@ -482,6 +488,8 @@
     ex["f0"].stage(get_source)
     ex["f0"].start()
 
+    for name in ex:
+        ex[name].clear_absent()
     for level in levels:
         level.clear()
 
@@ -575,6 +583,8 @@
         if field >= 3:
             putter(*three(l2.xa))(field - 3, i, r0, value)
 
+    for name in ("c0", "f0", "c1", "c2", "f1"):
+        ex[name].finish_send()
     ex["f2"].finish(put_f2)
     ex["x1"].start()
     l2.smooth_down(4)
@@ -653,24 +663,27 @@
     ex["y2"].stage(getter(*three(l2.xa)))
     ex["y2"].start()
     ex["x1"].finish(putter(*three(l1.xb)))
+
+    def sent(n, carry):
+        gather_copy(n).wait_send()
+        return carry
+
+    lax.fori_loop(1, devices, sent, 0)
+    for name in ("f2", "x1", "x2"):
+        ex[name].finish_send()
     ex["y2"].finish(putter(*three(l2.xa)))
     l1.add_grown(l2.xa, 0, 0, temp)
     up(l1)
     ex["y1"].stage(getter(*three(l1.xa)))
     ex["y1"].start()
     ex["x0"].finish(putter(*three(l0.xb)))
+    ex["x0"].finish_send()
+    ex["y2"].finish_send()
     ex["y1"].finish(putter(*three(l1.xa)))
     l0.add_grown(l1.xa, 0, 0, temp)
     up(l0, out)
 
-    for name in ex:
-        ex[name].finish_send()
-
-    def sent(n, carry):
-        gather_copy(n).wait_send()
-        return carry
-
-    lax.fori_loop(1, devices, sent, 0)
+    ex["y1"].finish_send()
 
 
 def up(level, out=None):

time: 69.7 us -> 73.9 us (1.060)
  Pallas kernels: 67.7 us -> 71.8 us
    pallas_call x1, Pallas kernels: 67.7 us -> 71.8 us  [on_device(): pl.pallas_call(kernel, out_shape=jax.ShapeDtypeStruct(right_side.shape, j...]
where the time goes in v3:
time: 73.9 us; the launch traced here: 73.5 us
  Pallas kernels  71.8 us (97%)
  local copies, waits for them, and re-layouts  1.77 us (2%)
    pallas_call x1, Pallas kernels, on_device(): pl.pallas_call(kernel, out_shape=jax.ShapeDtypeStruct(right_side.shape, j...  71.8 us
    unnamed x1, local copies, waits for them, and re-layouts  1.77 us

profile of v3, /device:TPU:1, one launch (start us, length us, event | category | flops | bytes accessed | tf_op | source)
XLA Modules:
  0.0 73.5 jit_solution(18435173482805740880)
XLA Ops:
  0.0 71.8 %shard_map.37 = f32[3,16,16,128]{3,2,1,0:T(8,128)} custom-call(f32[3,16,16,128]{3,2,1,0:T(8,128)} %refs_0_.1, f32[16,16,128]{2,1,0:T(8,128)} %refs_1_.1, f32[16,16,128]{2,1,0:T(8,128)} %refs_2_.1), custom_call_target="tpu_custom_call" | custom-call | tf_op jit(solution)/shard_map/pallas_call | solution.py:718
  71.8 1.8 %copy.5 = f32[3,16,16,128]{3,2,1,0:T(8,128)} copy(f32[3,16,16,128]{3,2,1,0:T(8,128)} %shard_map.37) | data formatting | bytes 786432

commit v4 on v2

--- a/solution.py
+++ b/solution.py
@@ -96,6 +96,17 @@
         self.sx, self.sy, self.sc, self.rx, self.ry, self.rc, self.ssem, self.rsem = refs
         self.where = where
 
+    def corner(self, ex, ey):
+        rows, at = [], 0
+        for j in range(self.packed):
+            for field, width in enumerate(self.widths):
+                if ex == ey and self.group == 1:
+                    width -= j + 1 if ex < 0 else self.packed - j
+                if width > 0:
+                    rows.append((j, field, width, at))
+                    at += width
+        return rows, round8(at)
+
     def copy(self, ex, ey):
         g, b, _ = self.where
         if ey == 0:
@@ -106,7 +117,8 @@
             src, dst = self.sy.at[side], self.ry.at[1 - side]
         else:
             side = (1 if ex > 0 else 0) * 2 + (1 if ey > 0 else 0)
-            src, dst = self.sc.at[side], self.rc.at[3 - side]
+            rows = pl.ds(0, self.corner(ex, ey)[1])
+            src, dst = self.sc.at[side, rows], self.rc.at[3 - side, rows]
         return pltpu.make_async_remote_copy(
             src_ref=src,
             dst_ref=dst,
@@ -128,11 +140,13 @@
                     value = load(field, j, 0 if side == 0 else size - width, width)
                     at = j * self.width + self.offs[field]
                     self.sy[side, at : at + width, :] = value
-                    if j < self.packed:
-                        self.sc[side, at : at + width, :] = value
-                    if j >= last:
-                        at = (j - last) * self.width + self.offs[field]
-                        self.sc[2 + side, at : at + width, :] = value
+        for ex in (-1, 1):
+            for ey in (-1, 1):
+                side = (1 if ex > 0 else 0) * 2 + (1 if ey > 0 else 0)
+                for j, field, width, at in self.corner(ex, ey)[0]:
+                    r0 = 0 if ey < 0 else size - width
+                    value = load(field, j if ex < 0 else last + j, r0, width)
+                    self.sc[side, at : at + width, :] = value
         for side in (0, 1):
             for j in range(self.packed):
                 for field in range(len(self.widths)):
@@ -169,6 +183,12 @@
                 self.copy(-dx, -dy).wait_recv()
                 xside, yside = (0 if dx < 0 else 1), (0 if dy < 0 else 1)
                 base = {-1: -self.packed * group, 0: 0, 1: size}[dx]
+                if dx and dy:
+                    for j, field, width, at in self.corner(-dx, -dy)[0]:
+                        value = self.rc[2 * xside + yside, at : at + width, :]
+                        y0 = -width if dy < 0 else size
+                        spread_rows(value, base + j * group, field, y0)
+                    return
                 for j in range(self.packed if dx else self.blocks):
                     for field, width in enumerate(self.widths):
                         if dy == 0:
@@ -176,11 +196,7 @@
                             value, y0 = self.rx[xside, at : at + size, :], 0
                         else:
                             at = j * self.width + self.offs[field]
-                            rows = slice(at, at + width)
-                            if dx == 0:
-                                value = self.ry[yside, rows, :]
-                            else:
-                                value = self.rc[2 * xside + yside, rows, :]
+                            value = self.ry[yside, at : at + width, :]
                             y0 = -width if dy < 0 else size
                         spread_rows(value, base + j * group, field, y0)
 
@@ -271,12 +287,15 @@
         wm = slice(w0 - 1, w0 + wn - 1)
         wp = slice(w0 + 1, w0 + wn + 1)
 
+        def scaled(value):
+            return value if bs == 1.0 else bs * value
+
         def flat(i, rows, rows_next):
             total = src[0, i + 1, rows, :] - src[0, i, rows, :]
             return total + (src[1, i, rows_next, :] - src[1, i, rows, :])
 
         def div(part, uz, ahead):
-            return bs * (part + (jnp.where(last, 0.0, ahead) - uz))
+            return scaled(part + (jnp.where(last, 0.0, ahead) - uz))
 
         def one(i, before):
             u = [src[c, i, w, :] for c in range(3)]
@@ -286,7 +305,7 @@
             here = div(part, u[2], ahead[2])
             side_z = src[2, i, wm, :]
             beside = div(flat(i, wm, w), side_z, roll(side_z, -z))
-            under = bs * (u[2] + jnp.where(first, 0.0, roll(part - u[2], z)))
+            under = scaled(u[2] + jnp.where(first, 0.0, roll(part - u[2], z)))
             gradients = (before, beside, under)
             kxp, kxm = self.kx[i, w, :], self.kx[i - 1, w, :]
             kyp, kym = self.ky[i, w, :], self.ky[i, wm, :]
@@ -319,15 +338,13 @@
         rates = rate_list()
 
         def consume(i, w, u, au):
-            inv = self.inv[i, w, :]
+            gain = 1.0 / THETA if number == 0 else 2.0 * rates[number] / DELTA
+            inv = gain * self.inv[i, w, :]
             stores = []
             for c in range(3):
-                resid = self.f[c, i, w, :] - au[c]
-                if number == 0:
-                    p = (1.0 / THETA) * (inv * resid)
-                else:
-                    p = rates[number] * rates[number - 1] * self.p[c, i, w, :]
-                    p = p + (2.0 * rates[number] / DELTA) * (inv * resid)
+                p = inv * (self.f[c, i, w, :] - au[c])
+                if number:
+                    p = p + rates[number] * rates[number - 1] * self.p[c, i, w, :]
                 at = (c, i, w, slice(None))
                 if number < 3:
                     stores.append((self.p, at, p))
@@ -559,7 +576,6 @@
     own_prepare(l1, 4)
     own_prepare(l2, 4)
     ex["f1"].finish(putter(*three(l1.f)))
-    ex["x0"].start()
     l1.first_direction(4)
     l1.smooth_down(4)
     l1.residual()
@@ -575,8 +591,9 @@
         if field >= 3:
             putter(*three(l2.xa))(field - 3, i, r0, value)
 
+    for name in ("c0", "f0", "c1", "c2", "f1"):
+        ex[name].finish_send()
     ex["f2"].finish(put_f2)
-    ex["x1"].start()
     l2.smooth_down(4)
     ex["x2"].stage(getter(*three(l2.xb)))
     ex["x2"].start()
@@ -630,6 +647,8 @@
         return carry
 
     lax.fori_loop(1, devices, receive, 0)
+    ex["x1"].start()
+    ex["x0"].start()
     for og in range(groups):
         for field in range(5):
             value = slots[pl.ds(og * bricks * 8 + field, bricks, stride=8), :]
@@ -653,24 +672,27 @@
     ex["y2"].stage(getter(*three(l2.xa)))
     ex["y2"].start()
     ex["x1"].finish(putter(*three(l1.xb)))
+
+    def sent(n, carry):
+        gather_copy(n).wait_send()
+        return carry
+
+    lax.fori_loop(1, devices, sent, 0)
+    for name in ("f2", "x1", "x2"):
+        ex[name].finish_send()
     ex["y2"].finish(putter(*three(l2.xa)))
     l1.add_grown(l2.xa, 0, 0, temp)
     up(l1)
     ex["y1"].stage(getter(*three(l1.xa)))
     ex["y1"].start()
     ex["x0"].finish(putter(*three(l0.xb)))
+    ex["y2"].finish_send()
     ex["y1"].finish(putter(*three(l1.xa)))
     l0.add_grown(l1.xa, 0, 0, temp)
     up(l0, out)
 
-    for name in ex:
-        ex[name].finish_send()
-
-    def sent(n, carry):
-        gather_copy(n).wait_send()
-        return carry
-
-    lax.fori_loop(1, devices, sent, 0)
+    ex["x0"].finish_send()
+    ex["y1"].finish_send()
 
 
 def up(level, out=None):

time: 69.7 us -> 67.6 us (0.970)
  Pallas kernels: 67.7 us -> 65.7 us
    pallas_call x1, Pallas kernels: 67.7 us -> 65.7 us  [on_device(): pl.pallas_call(kernel, out_shape=jax.ShapeDtypeStruct(right_side.shape, j...]
where the time goes in v4:
time: 67.6 us; the launch traced here: 67.4 us
  Pallas kernels  65.7 us (97%)
  local copies, waits for them, and re-layouts  1.77 us (3%)
    pallas_call x1, Pallas kernels, on_device(): pl.pallas_call(kernel, out_shape=jax.ShapeDtypeStruct(right_side.shape, j...  65.7 us
    unnamed x1, local copies, waits for them, and re-layouts  1.77 us

profile of v4, /device:TPU:1, one launch (start us, length us, event | category | flops | bytes accessed | tf_op | source)
XLA Modules:
  0.0 67.4 jit_solution(1416135714212638976)
XLA Ops:
  0.0 65.7 %shard_map.37 = f32[3,16,16,128]{3,2,1,0:T(8,128)} custom-call(f32[3,16,16,128]{3,2,1,0:T(8,128)} %refs_0_.1, f32[16,16,128]{2,1,0:T(8,128)} %refs_1_.1, f32[16,16,128]{2,1,0:T(8,128)} %refs_2_.1), custom_call_target="tpu_custom_call" | custom-call | tf_op jit(solution)/shard_map/pallas_call | solution.py:727
  65.7 1.8 %copy.5 = f32[3,16,16,128]{3,2,1,0:T(8,128)} copy(f32[3,16,16,128]{3,2,1,0:T(8,128)} %shard_map.37) | data formatting | bytes 786432

commit v5 on v4

--- a/solution.py
+++ b/solution.py
@@ -13,6 +13,8 @@
 HY = 8
 LANES = 128
 DIRS = [(a, b) for a in (-1, 0, 1) for b in (-1, 0, 1) if (a, b) != (0, 0)]
+START = sorted(DIRS, key=lambda d: (d[1] == 0, d[0] != 0))
+FINISH = START[::-1]
 
 
 def rate_list():
@@ -156,7 +158,7 @@
 
     def start(self):
         exists = self.where[2]
-        for d in DIRS:
+        for d in START:
             @pl.when(exists[d])
             def _(d=d):
                 self.copy(*d).start()
@@ -176,7 +178,7 @@
             for t in range(group):
                 put(field, x0 + t, y0, unpack(value, group, t))
 
-        for d in DIRS:
+        for d in FINISH:
             @pl.when(exists[d])
             def _(d=d):
                 dx, dy = d

time: 67.6 us -> 66.1 us (0.978)
  Pallas kernels: 65.7 us -> 64 us
    pallas_call x1, Pallas kernels: 65.7 us -> 64 us  [on_device(): pl.pallas_call(kernel, out_shape=jax.ShapeDtypeStruct(right_side.shape, j...]
where the time goes in v5:
time: 66.1 us; the launch traced here: 65.8 us
  Pallas kernels  64 us (97%)
  local copies, waits for them, and re-layouts  1.77 us (3%)
    pallas_call x1, Pallas kernels, on_device(): pl.pallas_call(kernel, out_shape=jax.ShapeDtypeStruct(right_side.shape, j...  64 us
    unnamed x1, local copies, waits for them, and re-layouts  1.77 us

profile of v5, /device:TPU:1, one launch (start us, length us, event | category | flops | bytes accessed | tf_op | source)
XLA Modules:
  0.0 65.8 jit_solution(8159941636079143856)
XLA Ops:
  0.0 64.0 %shard_map.37 = f32[3,16,16,128]{3,2,1,0:T(8,128)} custom-call(f32[3,16,16,128]{3,2,1,0:T(8,128)} %refs_0_.1, f32[16,16,128]{2,1,0:T(8,128)} %refs_1_.1, f32[16,16,128]{2,1,0:T(8,128)} %refs_2_.1), custom_call_target="tpu_custom_call" | custom-call | tf_op jit(solution)/shard_map/pallas_call | solution.py:729
  64.0 1.8 %copy.5 = f32[3,16,16,128]{3,2,1,0:T(8,128)} copy(f32[3,16,16,128]{3,2,1,0:T(8,128)} %shard_map.37) | data formatting | bytes 786432
